TPU v7x, 512 devices: a whole 4x8x8 slice. The times are simulated.
512 devices in a mesh: fsdp: 64 (over y, x, core), tensor: 8 (over z).
Axes of the slice: x: 4, y: 8, z: 8, core: 2. Of those that a mesh axis runs over, the one named last changes fastest.
Arguments:
- grad: bfloat16 [16384, 8192], P('tensor', 'fsdp'), may hold values from -0.26953125 to 0.26953125
- owner: int32 [4, 8], replicated, may hold values from 0 to 7, each once within a row
- codes: int32 [2, 16384, 8192], P(None, 'tensor', 'fsdp'), may hold values from 0 to 15
- scale_ids: int32 [2, 128, 8192], P(None, 'tensor', 'fsdp'), may hold values from 0 to 15
- scale_table: float32 [16], replicated, may hold values from 0.1 to 1
Outputs:
- statistics: float32 [2, 16384, 8192], P(None, 'tensor', 'fsdp')
Inputs may be any that keep to these rules, and one draw needn't show every extreme that they name: Each row owner[c] holds every slot 0 to 7 once: block row r of block column c keeps its statistics at slot owner[c, r].
All inputs are finite; a program needn't handle non-finite values.
Results may differ from a plain program's by a relative error of at most 0.0003.
Values may be sent and summed in bfloat16 or wider, within the bound.
No kernel may reach another device: no remote copies, remote signals or barrier semaphores. Data moves between devices by JAX's collectives and lax.ppermute only.
A program may use at most 64 MiB of HBM per device.

v0:
```python
import jax
import jax.numpy as jnp
from jax import lax
from jax.sharding import PartitionSpec as P

B = 2048


def partner_2(value, axis, bit):
    mask = 2**bit
    pairs = [(source, source ^ mask) for source in range(lax.axis_size(axis))]
    return lax.ppermute(value, axis, pairs)


def left_part(slab_piece, member, piece_width):
    own_rows = lax.dynamic_slice_in_dim(slab_piece, member * piece_width, piece_width, 1)
    return jnp.einsum("sbj,scj->sbc", slab_piece, own_rows, preferred_element_type=jnp.float32)


def right_part(slab_piece, own_piece):
    return jnp.einsum("sbj,sbc->sjc", slab_piece, own_piece, preferred_element_type=jnp.float32)


def shards(grad, owner, codes, scale_ids, scale_table):
    rows_here = grad.shape[0]
    width_here = grad.shape[1]
    slot_count = rows_here // B
    tensor_count = lax.axis_size("tensor")
    group_size = B // width_here
    tensor_pos = lax.axis_index("tensor")
    fsdp_pos = lax.axis_index("fsdp")
    column_block = fsdp_pos // group_size
    member = fsdp_pos % group_size
    owner_row = lax.dynamic_index_in_dim(owner, column_block, 0, keepdims=False)
    pieces = grad.reshape(slot_count, B, width_here)
    local_slots = lax.dynamic_slice_in_dim(owner_row, tensor_pos * slot_count, slot_count)
    targets = jnp.arange(tensor_count * slot_count, dtype=jnp.int32).reshape(
        tensor_count, slot_count
    )
    select = (targets[:, :, None] == local_slots[None, None, :]).astype(jnp.bfloat16)
    outgoing = jnp.einsum(
        "dsr,rbc->dsbc", select, pieces, preferred_element_type=jnp.float32
    ).astype(jnp.bfloat16)
    incoming = lax.all_to_all(outgoing, "tensor", split_axis=0, concat_axis=0, tiled=True)
    owned_block = jnp.sum(incoming, axis=0, dtype=jnp.float32).astype(jnp.bfloat16)
    depth_count = group_size.bit_length() - 1
    collected = owned_block
    for step_bit in range(depth_count):
        partner = partner_2(collected, "fsdp", step_bit)
        upper_half = fsdp_pos // (1 << step_bit) % 2 == 1
        collected = jnp.where(
            upper_half,
            jnp.concatenate([partner, collected], 2),
            jnp.concatenate([collected, partner], 2),
        )
    left_gram = left_part(collected, member, width_here)
    right_gram = right_part(collected, owned_block)
    stacked = jnp.stack(
        [left_gram.reshape(rows_here, width_here), right_gram.reshape(rows_here, width_here)]
    )
    group_rows = rows_here // scale_ids.shape[1]
    level_index = jnp.arange(scale_table.shape[0], dtype=jnp.int32)
    scale_grid = jnp.sum(jnp.where(scale_ids[..., None] == level_index, scale_table, 0.0), axis=-1)
    previous = scale_grid[:, :, None, :] * (
        (codes.reshape(2, -1, group_rows, width_here).astype(jnp.float32) - 7.5) / 7.5
    )
    previous = previous.reshape(2, rows_here, width_here)
    return 0.9 * previous + 0.1 * stacked


def solution(mesh):
    in_specs = (P("tensor", "fsdp"), P(), P(None, "tensor", "fsdp"), P(None, "tensor", "fsdp"), P())
    out_specs = P(None, "tensor", "fsdp")
    return jax.shard_map(shards, mesh=mesh, in_specs=in_specs, out_specs=out_specs, check_vma=False)
```

profile of v0, /device:TPU:1, one launch (start us, length us, event | category | flops | bytes accessed | tf_op | source)
XLA Modules:
  0.0 311.6 jit_solution(14582785439672155891)
XLA Ops:
  0.0 1.1 convert.8
  1.1 1.3 dynamic_slice.8
  2.4 0.6 compare_convert_fusion
  3.1 0.7 fusion
  3.8 105.4 %all_to_all.5 = bf16[8,1,2048,128]{3,2,1,0:T(8,128)(2,1)} all-to-all(bf16[8,1,2048,128]{3,2,1,0:T(8,128)(2,1)S(1)} %fusion), channel_id=1, replica_groups=mesh['fsdp'=64,'tensor'=8] {'tensor'}, dimensions={0} | all-to-all | bytes 8388608 | tf_op jit(solution)/shard_map/all_to_all | solution.py:44
  109.2 3.1 reduce_sum.24
  112.3 0.0 copy-start
  112.3 4.4 %collective-permute-start = (bf16[1,2048,128]{2,1,0:T(8,128)(2,1)S(1)}, bf16[1,2048,128]{2,1,0:T(8,128)(2,1)S(1)}, u32[]{:S(2)}, u32[]{:S(2)}) collective-permute-start(bf16[1,2048,128]{2,1,0:T(8,128)(2,1)S(1)} %bitcast.27), channel_id=1, source_target_pairs={{0,8},{8,0},{16,24},{24,16},{32,40},{40,32},{48,56},{56,48},{64,72... | collective-permute-start | bytes 1572872 | tf_op jit(solution)/shard_map/ppermute | solution.py:12
  116.7 1.5 collective-permute-done
  118.2 1.3 maximum_select_fusion.7
  119.5 3.1 collective-permute-start.1
  122.6 0.4 maximum_select_fusion.8
  123.0 22.9 %collective-permute-done.1 = bf16[1,2048,256]{2,1,0:T(8,128)(2,1)S(1)} collective-permute-done((bf16[1,2048,256]{2,1,0:T(8,128)(2,1)}, bf16[1,2048,256]{2,1,0:T(8,128)(2,1)S(1)}, u32[]{:S(2)}, u32[]{:S(2)}) %collective-permute-start.1) | collective-permute-done | bytes 1048608 | tf_op jit(solution)/shard_map/ppermute | solution.py:12
  146.0 0.0 copy-start.2
  146.0 1.8 maximum_select_fusion.3
  147.8 0.0 copy-done
  147.8 4.6 %collective-permute-start.2 = (bf16[1,2048,512]{2,1,0:T(8,128)(2,1)}, bf16[1,2048,512]{2,1,0:T(8,128)(2,1)}, u32[]{:S(2)}, u32[]{:S(2)}) collective-permute-start(bf16[1,2048,512]{2,1,0:T(8,128)(2,1)} %maximum_select_fusion.3), channel_id=1, source_target_pairs={{0,32},{8,40},{16,48},{24,56},{32,0},{40,8},{48,16},{56,24},{64,96... | collective-permute-start | bytes 6291464 | tf_op jit(solution)/shard_map/ppermute | solution.py:12
  152.4 0.0 copy-done.2
  152.5 2.0 maximum_select_fusion.4
  154.5 42.9 %collective-permute-done.2 = bf16[1,2048,512]{2,1,0:T(8,128)(2,1)} collective-permute-done((bf16[1,2048,512]{2,1,0:T(8,128)(2,1)}, bf16[1,2048,512]{2,1,0:T(8,128)(2,1)}, u32[]{:S(2)}, u32[]{:S(2)}) %collective-permute-start.2) | collective-permute-done | bytes 2097184 | tf_op jit(solution)/shard_map/ppermute | solution.py:12
  197.4 0.0 copy-start.4
  197.4 0.0 copy-start.5
  197.4 5.1 %maximum_select_fusion.1 = bf16[1,2048,1024]{2,1,0:T(8,128)(2,1)} fusion(bf16[1,2048,512]{2,1,0:T(8,128)(2,1)S(1)} %bitcast.25, bf16[1,2048,512]{2,1,0:T(8,128)(2,1)} %collective-permute-done.2, pred[]{:T(512)S(6)} %eq.52), kind=kLoop, calls=%fused_computation.7 | loop fusion | flops 18874368 | bytes 8388609 | tf_op jit(solution)/shard_map/jit(_where)/select_n | solution.py:51
  202.5 3.2 %collective-permute-start.3 = (bf16[1,2048,1024]{2,1,0:T(8,128)(2,1)}, bf16[1,2048,1024]{2,1,0:T(8,128)(2,1)}, u32[]{:S(2)}, u32[]{:S(2)}) collective-permute-start(bf16[1,2048,1024]{2,1,0:T(8,128)(2,1)} %maximum_select_fusion.1), channel_id=1, source_target_pairs={{0,64},{8,72},{16,80},{24,88},{32,96},{40,104},{48,112},{56,120},{... | collective-permute-start | bytes 12582920 | tf_op jit(solution)/shard_map/ppermute | solution.py:12
  205.7 0.0 copy-done.4
  205.7 0.0 copy-done.5
  205.7 0.1 select_reduce_fusion
  205.9 0.0 copy-start.1
  205.9 3.7 %maximum_select_fusion.2 = bf16[2048,1024]{1,0:T(8,128)(2,1)S(1)} fusion(bf16[2048,512]{1,0:T(8,128)(2,1)S(1)} %maximum_select_fusion.4, bf16[2048,512]{1,0:T(8,128)(2,1)} %bitcast.9, pred[]{:T(512)S(6)} %eq.52), kind=kLoop, calls=%fused_computation.8 | loop fusion | flops 18874368 | bytes 8388609 | tf_op jit(solution)/shard_map/jit(_where)/select_n | solution.py:51
  209.5 85.1 %collective-permute-done.3 = bf16[1,2048,1024]{2,1,0:T(8,128)(2,1)} collective-permute-done((bf16[1,2048,1024]{2,1,0:T(8,128)(2,1)}, bf16[1,2048,1024]{2,1,0:T(8,128)(2,1)}, u32[]{:S(2)}, u32[]{:S(2)}) %collective-permute-start.3) | collective-permute-done | bytes 4194336 | tf_op jit(solution)/shard_map/ppermute | solution.py:12
  294.6 0.0 copy-done.1
  294.6 8.8 %convolution_bitcast_fusion = f32[1,2048,128]{2,1,0:T(8,128)S(1)} fusion(bf16[2048,128]{1,0:T(8,128)(2,1)S(1)} %copy-done.1, bf16[2048,1024]{1,0:T(8,128)(2,1)S(1)} %maximum_select_fusion.2, bf16[2048,1024]{1,0:T(8,128)(2,1)} %bitcast.8, pred[]{:T(512)S(6)} %eq.51), kind=kOutput, calls=%fused_computation.9 | convolution fusion | flops 1111490560 | bytes 9961473 | tf_op jit(solution)/shard_map/sbj,sbc->sjc/dot_general | solution.py:21
  303.4 0.0 copy-start.3
  303.4 6.4 %convolution_bitcast_fusion.1 = f32[1,2048,128]{2,1,0:T(8,128)S(1)} fusion(bf16[2048,1024]{1,0:T(8,128)(2,1)S(1)} %maximum_select_fusion.2, bf16[2048,1024]{1,0:T(8,128)(2,1)} %bitcast.8, pred[]{:T(512)S(6)} %eq.51, s32[]{:T(128)S(6)} %select_n.200, bf16[1,2048,1024]{2,1,0:T(8,128)(2,1)} %collective-permute-done.3, bf16[1,2048,1024]{2,1,0:T(8,128)(2,1)S(1)} %bitcast.30), kind=kOutput, calls=%fused_computation.10 | convolution fusion | flops 1113849856 | bytes 17827328 | tf_op jit(solution)/shard_map/sbj,scj->sbc/dot_general | solution.py:17
  309.9 0.0 copy-done.3
  309.9 1.7 fusion.1
  (1 shorter events, 0.0 us)
Async XLA Ops:
  112.3 35.5 %copy-start = (bf16[2048,128]{1,0:T(8,128)(2,1)}, bf16[2048,128]{1,0:T(8,128)(2,1)S(1)}, u32[]{:S(2)}) copy-start(bf16[2048,128]{1,0:T(8,128)(2,1)S(1)} %reduce_sum.24) | copy-start | bytes 1572868
  112.3 5.9 %collective-permute-start = (bf16[1,2048,128]{2,1,0:T(8,128)(2,1)S(1)}, bf16[1,2048,128]{2,1,0:T(8,128)(2,1)S(1)}, u32[]{:S(2)}, u32[]{:S(2)}) collective-permute-start(bf16[1,2048,128]{2,1,0:T(8,128)(2,1)S(1)} %bitcast.27), channel_id=1, source_target_pairs={{0,8},{8,0},{16,24},{24,16},{32,40},{40,32},{48,56},{56,48},{64,72... | collective-permute-start | bytes 1572872 | tf_op jit(solution)/shard_map/ppermute | solution.py:12
  119.5 26.5 %collective-permute-start.1 = (bf16[1,2048,256]{2,1,0:T(8,128)(2,1)}, bf16[1,2048,256]{2,1,0:T(8,128)(2,1)S(1)}, u32[]{:S(2)}, u32[]{:S(2)}) collective-permute-start(bf16[1,2048,256]{2,1,0:T(8,128)(2,1)} %maximum_select_fusion.7), channel_id=1, source_target_pairs={{0,16},{8,24},{16,0},{24,8},{32,48},{40,56},{48,32},{56,40},{64,80... | collective-permute-start | bytes 3145736 | tf_op jit(solution)/shard_map/ppermute | solution.py:12
  146.0 6.5 %copy-start.2 = (bf16[1,2048,256]{2,1,0:T(8,128)(2,1)}, bf16[1,2048,256]{2,1,0:T(8,128)(2,1)S(1)}, u32[]{:S(2)}) copy-start(bf16[1,2048,256]{2,1,0:T(8,128)(2,1)S(1)} %collective-permute-done.1) | copy-start | bytes 3145732
  147.8 49.6 %collective-permute-start.2 = (bf16[1,2048,512]{2,1,0:T(8,128)(2,1)}, bf16[1,2048,512]{2,1,0:T(8,128)(2,1)}, u32[]{:S(2)}, u32[]{:S(2)}) collective-permute-start(bf16[1,2048,512]{2,1,0:T(8,128)(2,1)} %maximum_select_fusion.3), channel_id=1, source_target_pairs={{0,32},{8,40},{16,48},{24,56},{32,0},{40,8},{48,16},{56,24},{64,96... | collective-permute-start | bytes 6291464 | tf_op jit(solution)/shard_map/ppermute | solution.py:12
  197.4 8.3 %copy-start.4 = (s32[2,16,128]{2,1,0:T(8,128)S(1)}, s32[2,16,128]{2,1,0:T(8,128)}, u32[]{:S(2)}) copy-start(s32[2,16,128]{2,1,0:T(8,128)} %param.8) | copy-start | bytes 49156
  197.4 8.3 %copy-start.5 = (f32[16]{0:T(128)S(1)}, f32[16]{0:T(128)}, u32[]{:S(2)}) copy-start(f32[16]{0:T(128)} %param.9) | copy-start | bytes 196
  202.5 92.1 %collective-permute-start.3 = (bf16[1,2048,1024]{2,1,0:T(8,128)(2,1)}, bf16[1,2048,1024]{2,1,0:T(8,128)(2,1)}, u32[]{:S(2)}, u32[]{:S(2)}) collective-permute-start(bf16[1,2048,1024]{2,1,0:T(8,128)(2,1)} %maximum_select_fusion.1), channel_id=1, source_target_pairs={{0,64},{8,72},{16,80},{24,88},{32,96},{40,104},{48,112},{56,120},{... | collective-permute-start | bytes 12582920 | tf_op jit(solution)/shard_map/ppermute | solution.py:12
  205.9 88.7 %copy-start.1 = (bf16[2048,128]{1,0:T(8,128)(2,1)S(1)}, bf16[2048,128]{1,0:T(8,128)(2,1)}, u32[]{:S(2)}) copy-start(bf16[2048,128]{1,0:T(8,128)(2,1)} %copy-done) | copy-start | bytes 1572868
  303.4 6.4 %copy-start.3 = (s32[2,2048,128]{2,1,0:T(8,128)S(1)}, s32[2,2048,128]{2,1,0:T(8,128)}, u32[]{:S(2)}) copy-start(s32[2,2048,128]{2,1,0:T(8,128)} %param.7) | copy-start | bytes 6291460
where the time goes:
time: 313 us; the launch traced here: 312 us
  waiting for transfers between devices  152 us (49%)
  blocking collectives  105 us (34%)
  other arithmetic  21.7 us (7%)
  starting transfers between devices  15.3 us (5%)
  matrix products  15.2 us (5%)
    ppermute x4, waiting for transfers between devices, partner_2(): return lax.ppermute(value, axis, pairs)  152 us
    all_to_all x1, blocking collectives, shards(): lax.all_to_all(outgoing, 'tensor', split_axis=0, concat_axis=0, tiled=True)  105 us
    ppermute x4, starting transfers between devices, partner_2(): return lax.ppermute(value, axis, pairs)  15.3 us
    select_n x6, other arithmetic, shards(): jnp.where(upper_half, jnp.concatenate([partner, collected], 2), jnp.conca...  14.3 us
    dot_general x1, matrix products, right_part(): jnp.einsum('sbj,sbc->sjc', slab_piece, own_piece, preferred_element_type=...  8.82 us
    dot_general x1, matrix products, left_part(): jnp.einsum('sbj,scj->sbc', slab_piece, own_rows, preferred_element_type=j...  6.4 us
  transfers between devices with their start and end apart: 4, of which 4 were waited for; matrix products, arithmetic and copies ran while one was open for 2% of the time, Pallas kernels for 0%

commit v1 on v0

v1 whole, which is shorter than its diff:
```python
import functools

import jax
import jax.numpy as jnp
from jax import lax
from jax.experimental import pallas as pl
from jax.experimental.pallas import tpu as pltpu
from jax.sharding import Mesh
from jax.sharding import PartitionSpec as P

B = 2048
PLANE = ("y", "x", "core")


def place_kernel(owner_ref, block_ref, in_ref, out_ref):
    column_block = block_ref[0]
    for row_block in range(in_ref.shape[0]):
        slot = owner_ref[column_block, row_block]
        out_ref[pl.ds(slot, 1)] = in_ref[row_block : row_block + 1]


def place(chunks, owner, column_block):
    return pl.pallas_call(
        place_kernel,
        out_shape=jax.ShapeDtypeStruct(chunks.shape, chunks.dtype),
        in_specs=[
            pl.BlockSpec(memory_space=pltpu.SMEM),
            pl.BlockSpec(memory_space=pltpu.SMEM),
            pl.BlockSpec(memory_space=pltpu.VMEM),
        ],
        out_specs=pl.BlockSpec(memory_space=pltpu.VMEM),
    )(owner, column_block, chunks)


def shards(grad, owner, codes, scale_ids, scale_table):
    rows_here, width_here = grad.shape
    slots = lax.axis_size("tensor")
    column_block = lax.axis_index("c")
    member = lax.axis_index(PLANE)
    chunks = grad.reshape(slots, rows_here // slots, width_here)
    spread = lax.all_to_all(chunks, "tensor", 0, 0, tiled=True)
    placed = place(spread, owner, column_block.reshape(1))
    own = lax.all_to_all(placed, "tensor", 0, 0, tiled=True).reshape(rows_here, width_here)
    pieces = lax.all_gather(own, PLANE, axis=0)
    own_rows = lax.dynamic_slice_in_dim(pieces, member * width_here, width_here, 1)
    left = jnp.einsum("nkc,nic->ki", pieces, own_rows, preferred_element_type=jnp.float32)
    right = jnp.einsum("nkc,kd->ncd", pieces, own, preferred_element_type=jnp.float32)
    stacked = jnp.stack([left, right.reshape(rows_here, width_here)])
    group_rows = rows_here // scale_ids.shape[1]
    level_index = jnp.arange(scale_table.shape[0], dtype=jnp.int32)
    scale_grid = jnp.sum(jnp.where(scale_ids[..., None] == level_index, scale_table, 0.0), axis=-1)
    previous = scale_grid[:, :, None, :] * (
        (codes.reshape(2, -1, group_rows, width_here).astype(jnp.float32) - 7.5) / 7.5
    )
    return 0.9 * previous.reshape(2, rows_here, width_here) + 0.1 * stacked


def solution(mesh):
    fine = Mesh(
        mesh.devices.reshape(4, 2, 4, 2, 8), ("c", "y", "x", "core", "tensor")
    )
    fsdp = ("c", "y", "x", "core")
    in_specs = (P("tensor", fsdp), P(), P(None, "tensor", fsdp), P(None, "tensor", fsdp), P())
    out_specs = P(None, "tensor", fsdp)
    return jax.shard_map(shards, mesh=fine, in_specs=in_specs, out_specs=out_specs, check_vma=False)
```

time: 313 us -> 144 us (0.46)
  blocking collectives: 105 us -> 21.9 us
  waiting for transfers between devices: 152 us -> 72 us
  other arithmetic: 21.7 us -> 1.86 us
  between operations: 0.29 us -> 13.5 us
  local copies, waits for them, and re-layouts: 1.3 us -> 13.1 us
  matrix products: 15.2 us -> 8.3 us
  starting transfers between devices: 15.3 us -> 11 us
    ppermute x4 -> x0, waiting for transfers between devices: 152 us -> none  [partner_2(): return lax.ppermute(value, axis, pairs)]
    all_to_all x1, blocking collectives: 105 us -> 21.9 us  [shards(): lax.all_to_all(placed, 'tensor', 0, 0, tiled=True)]
    all_gather x0 -> x1, waiting for transfers between devices: none -> 54.1 us  [shards(): pieces = lax.all_gather(own, PLANE, axis=0)]
    all_to_all x0 -> x1, waiting for transfers between devices: none -> 17.9 us  [shards(): spread = lax.all_to_all(chunks, 'tensor', 0, 0, tiled=True)]
    ppermute x4 -> x0, starting transfers between devices: 15.3 us -> none  [partner_2(): return lax.ppermute(value, axis, pairs)]
    select_n x6 -> x0, other arithmetic: 14.3 us -> none  [shards(): jnp.where(upper_half, jnp.concatenate([partner, collected], 2), jnp.conca...]
    all_gather x0 -> x1, local copies, waits for them, and re-layouts: none -> 12.3 us  [shards(): pieces = lax.all_gather(own, PLANE, axis=0)]
    all_to_all x0 -> x1, starting transfers between devices: none -> 11 us  [shards(): spread = lax.all_to_all(chunks, 'tensor', 0, 0, tiled=True)]
  transfers between devices with their start and end apart: 4 -> 2, of which waited for: 4 -> 2; matrix products, arithmetic and copies ran while one was open for 2% -> 0% of each run, Pallas kernels for 0% -> 0%
where the time goes in v1:
time: 144 us
  waiting for transfers between devices  72 us (50%)
  blocking collectives  21.9 us (15%)
  between operations  13.5 us (9%)
  local copies, waits for them, and re-layouts  13.1 us (9%)
  starting transfers between devices  11 us (8%)
  matrix products  8.3 us (6%)
  Pallas kernels  1.89 us (1%)
  other arithmetic  1.86 us (1%)
    all_gather x1, waiting for transfers between devices, shards(): pieces = lax.all_gather(own, PLANE, axis=0)  54.1 us
    all_to_all x1, blocking collectives, shards(): lax.all_to_all(placed, 'tensor', 0, 0, tiled=True)  21.9 us
    all_to_all x1, waiting for transfers between devices, shards(): spread = lax.all_to_all(chunks, 'tensor', 0, 0, tiled=True)  17.9 us
    all_gather x1, local copies, waits for them, and re-layouts, shards(): pieces = lax.all_gather(own, PLANE, axis=0)  12.3 us
    all_to_all x1, starting transfers between devices, shards(): spread = lax.all_to_all(chunks, 'tensor', 0, 0, tiled=True)  11 us
    dot_general x1, matrix products, shards(): jnp.einsum('nkc,kd->ncd', pieces, own, preferred_element_type=jnp.float32)  5.91 us
  transfers between devices with their start and end apart: 2, of which 2 were waited for; matrix products, arithmetic and copies ran while one was open for 0% of the time, Pallas kernels for 0%

profile of v1, /device:TPU:1, one launch (start us, length us, event | category | flops | bytes accessed | tf_op | source)
XLA Modules:
  0.0 143.5 jit_solution(10733796766589113384)
XLA Ops:
  6.5 0.0 copy-start.4
  6.5 0.0 copy-start.5
  6.5 11.0 %all-to-all-start = ((bf16[8,256,128]{2,1,0:T(8,128)(2,1)}), bf16[8,256,128]{2,1,0:T(8,128)(2,1)S(1)}, u32[]{:S(2)}, u32[]{:S(2)}) async-start(bf16[8,256,128]{2,1,0:T(8,128)(2,1)} %bitcast.24), calls=%async_computation | async-start | bytes 1048576 | tf_op jit(solution)/shard_map/all_to_all | solution.py:41
  17.5 0.0 all-gather.2.cloned.1.call-start
  17.6 17.9 %all-to-all-done.in_ref = bf16[8,256,128]{2,1,0:T(8,128)(2,1)S(1)} async-done(((bf16[8,256,128]{2,1,0:T(8,128)(2,1)}), bf16[8,256,128]{2,1,0:T(8,128)(2,1)S(1)}, u32[]{:S(2)}, u32[]{:S(2)}) %all-to-all-start) | async-done | bytes 524320 | tf_op jit(solution)/shard_map/all_to_all | solution.py:41
  35.5 0.0 copy-start.3
  35.5 0.8 copy-done.3
  36.3 1.9 %shard_map.55 = bf16[8,256,128]{2,1,0:T(8,128)(2,1)} custom-call(s32[4,8]{1,0:T(4,128)} %owner_ref.1, s32[1]{0:T(128)} %bitcast.1.block_ref, bf16[8,256,128]{2,1,0:T(8,128)(2,1)} %copy-done.3), custom_call_target="tpu_custom_call" | custom-call | tf_op jit(solution)/shard_map/pallas_call | solution.py:23
  38.2 21.9 %all_to_all.10 = bf16[8,256,128]{2,1,0:T(8,128)(2,1)} all-to-all(bf16[8,256,128]{2,1,0:T(8,128)(2,1)} %shard_map.55), channel_id=1, replica_groups=mesh['c'=4,'y'=2,'x'=4,'core'=2,'tensor'=8] {'tensor'}, dimensions={0} | all-to-all | bytes 1048576 | tf_op jit(solution)/shard_map/all_to_all | solution.py:43
  60.0 0.0 all-gather.2.cloned.1.call-update
  60.1 0.0 copy-done.4
  60.1 0.0 copy-done.5
  60.1 0.1 select_reduce_fusion
  60.2 0.0 copy-start.2
  60.2 54.1 %all-gather.2.cloned.1.call-done = bf16[16,2048,128]{2,1,0:T(8,128)(2,1)} async-done(((bf16[1,2048,128]{2,1,0:T(8,128)(2,1)}), bf16[16,2048,128]{2,1,0:T(8,128)(2,1)}) %all-gather.2.cloned.1.call-update) | async-done | bytes 8388624 | tf_op jit(solution)/shard_map/all_gather | solution.py:44
  114.3 12.3 %copy.8 = bf16[16,2048,128]{1,2,0:T(8,128)(2,1)} copy(bf16[16,2048,128]{2,1,0:T(8,128)(2,1)} %all-gather.2.cloned.1.call-done) | data formatting | bytes 16777216 | tf_op jit(solution)/shard_map/all_gather | solution.py:44
  126.6 0.0 copy-done.2
  126.6 0.0 copy-start
  126.6 5.9 %convolution_bitcast_fusion = f32[1,2048,128]{2,1,0:T(8,128)S(1)} fusion(bf16[2048,2048]{1,0:T(8,128)(2,1)} %bitcast.21, bf16[2048,128]{1,0:T(8,128)(2,1)S(1)} %bitcast.23), kind=kOutput, calls=%fused_computation | convolution fusion | flops 1073741824 | bytes 9961472 | tf_op jit(solution)/shard_map/nkc,kd->ncd/dot_general | solution.py:47
  132.5 0.0 copy-done
  132.5 0.0 copy-start.1
  132.5 2.4 %convolution_bitcast_fusion.1 = f32[1,2048,128]{2,1,0:T(8,128)S(1)} fusion(bf16[16,2048,128]{2,1,0:T(8,128)(2,1)S(1)} %copy-done, s32[]{:T(128)S(6)} %select_n.8), kind=kOutput, calls=%fused_computation.1 | convolution fusion | flops 1073741824 | bytes 9961476 | tf_op jit(solution)/shard_map/nkc,nic->ki/dot_general | solution.py:46
  134.9 0.0 copy-done.1
  134.9 1.7 %fusion = f32[2,2048,128]{2,1,0:T(8,128)} fusion(f32[1,2048,128]{2,1,0:T(8,128)S(1)} %convolution_bitcast_fusion, f32[1,2048,128]{2,1,0:T(8,128)S(1)} %convolution_bitcast_fusion.1, s32[2,2048,128]{2,1,0:T(8,128)S(1)} %copy-done.1, f32[2,16,128]{2,1,0:T(8,128)S(1)} %broadcast_multiply_fusion), kind=kLoop, calls=%fused_computation.3 | loop fusion | flops 3670016 | bytes 6307840 | tf_op jit(solution)/shard_map/add | solution.py:55
  (1 shorter events, 0.0 us)
Async XLA Ops:
  6.5 53.5 %copy-start.4 = (s32[2,16,128]{2,1,0:T(8,128)S(1)}, s32[2,16,128]{2,1,0:T(8,128)}, u32[]{:S(2)}) copy-start(s32[2,16,128]{2,1,0:T(8,128)} %param.8) | copy-start | bytes 49156
  6.5 53.5 %copy-start.5 = (f32[16]{0:T(128)S(1)}, f32[16]{0:T(128)}, u32[]{:S(2)}) copy-start(f32[16]{0:T(128)} %param.9) | copy-start | bytes 196
  6.5 29.0 %all-to-all-start = ((bf16[8,256,128]{2,1,0:T(8,128)(2,1)}), bf16[8,256,128]{2,1,0:T(8,128)(2,1)S(1)}, u32[]{:S(2)}, u32[]{:S(2)}) async-start(bf16[8,256,128]{2,1,0:T(8,128)(2,1)} %bitcast.24), calls=%async_computation | async-start | bytes 1048576 | tf_op jit(solution)/shard_map/all_to_all | solution.py:41
  17.5 96.8 %all-gather.2.cloned.1.call-start = ((), (), s32[]{:S(2)}) async-start(), calls=%async_computation.2 | async-start | bytes 8912896 | tf_op jit(solution)/shard_map/all_gather | solution.py:44
  35.5 0.8 copy-start.3
  60.2 66.4 %copy-start.2 = (bf16[8,256,128]{2,1,0:T(8,128)(2,1)S(1)}, bf16[8,256,128]{2,1,0:T(8,128)(2,1)}, u32[]{:S(2)}) copy-start(bf16[8,256,128]{2,1,0:T(8,128)(2,1)} %all_to_all.10) | copy-start | bytes 1572868
  126.6 5.9 %copy-start = (bf16[16,2048,128]{2,1,0:T(8,128)(2,1)S(1)}, bf16[16,2048,128]{2,1,0:T(8,128)(2,1)}, u32[]{:S(2)}) copy-start(bf16[16,2048,128]{2,1,0:T(8,128)(2,1)} %all-gather.2.cloned.1.call-done) | copy-start | bytes 25165828
  132.5 2.4 %copy-start.1 = (s32[2,2048,128]{2,1,0:T(8,128)S(1)}, s32[2,2048,128]{2,1,0:T(8,128)}, u32[]{:S(2)}) copy-start(s32[2,2048,128]{2,1,0:T(8,128)} %param.7) | copy-start | bytes 6291460
Sparse Core Ops, SparseCore 0:
  60.2 54.0 all-gather.1

commit v2 on v1

v2 whole, which is shorter than its diff:
```python
import functools

import jax
import jax.numpy as jnp
from jax import lax
from jax.experimental import pallas as pl
from jax.experimental.pallas import tpu as pltpu
from jax.sharding import Mesh
from jax.sharding import PartitionSpec as P

B = 2048
W = 128
CHIPS = 8
VMEM = pl.BlockSpec(memory_space=pltpu.VMEM)
SMEM = pl.BlockSpec(memory_space=pltpu.SMEM)
PARAMS = pltpu.CompilerParams(vmem_limit_bytes=40 * 2**20)
f32 = jnp.float32
bf16 = jnp.bfloat16


def place_kernel(owner_ref, block_ref, in_ref, out_ref):
    column_block = block_ref[0]
    for row_block in range(in_ref.shape[0]):
        slot = owner_ref[column_block, row_block]
        out_ref[pl.ds(slot, 1)] = in_ref[row_block : row_block + 1]


def place(chunks, owner, column_block):
    return pl.pallas_call(
        place_kernel,
        out_shape=jax.ShapeDtypeStruct(chunks.shape, chunks.dtype),
        in_specs=[SMEM, SMEM, VMEM],
        out_specs=VMEM,
        compiler_params=PARAMS,
    )(owner, column_block, chunks)


def dequant_kernel(table_ref, codes_ref, ids_ref, out_ref):
    ids = ids_ref[...]
    scale = jnp.zeros(ids.shape, f32)
    for level in range(table_ref.shape[0]):
        scale = jnp.where(ids == level, table_ref[level], scale)
    group_rows = codes_ref.shape[1] // ids.shape[1]
    for side in range(2):
        for group in range(ids.shape[1]):
            rows = slice(group * group_rows, (group + 1) * group_rows)
            code = codes_ref[side, rows, :].astype(f32)
            out_ref[side, rows, :] = 0.9 * (scale[side, group : group + 1] * ((code - 7.5) / 7.5))


def dequant(scale_table, codes, scale_ids):
    return pl.pallas_call(
        dequant_kernel,
        out_shape=jax.ShapeDtypeStruct(codes.shape, f32),
        in_specs=[SMEM, VMEM, VMEM],
        out_specs=VMEM,
        compiler_params=PARAMS,
        cost_estimate=pl.CostEstimate(flops=2**22, bytes_accessed=2**22, transcendentals=0),
    )(scale_table, codes, scale_ids)


def gram_kernel(at_ref, own_ref, other_ref, *refs):
    pieces, (keep_ref, send_ref, block, pair, rows) = refs[:CHIPS], refs[CHIPS:]
    own_row = pl.multiple_of(at_ref[0], W)
    other_row = pl.multiple_of(at_ref[1], W)
    for i, piece in enumerate(pieces):
        block[:, i * W : (i + 1) * W] = piece[...]
    pair[:, :W] = own_ref[...]
    pair[:, W:] = other_ref[...]
    rows[:W, :] = block[pl.ds(own_row, W), :]
    rows[W:, :] = block[pl.ds(other_row, W), :]
    for start in range(0, B, 512):
        left = lax.dot_general(
            block[start : start + 512, :],
            rows[...],
            (((1,), (1,)), ((), ())),
            preferred_element_type=f32,
        )
        keep_ref[start : start + 512, :] = left[:, :W]
        send_ref[start : start + 512, :] = left[:, W:]
    for i in range(0, CHIPS, 2):
        right = lax.dot_general(
            block[:, i * W : (i + 2) * W],
            pair[...],
            (((0,), (0,)), ((), ())),
            preferred_element_type=f32,
        )
        for j in range(2):
            start = pl.multiple_of(at_ref[2 + i + j], W)
            keep_ref[pl.ds(start, W), :] = right[j * W : (j + 1) * W, :W]
            send_ref[pl.ds(start, W), :] = right[j * W : (j + 1) * W, W:]


def grams(at, own, other, pieces):
    out = jax.ShapeDtypeStruct((B + CHIPS * W, W), f32)
    return pl.pallas_call(
        gram_kernel,
        out_shape=(out, out),
        in_specs=[SMEM] + [VMEM] * (2 + CHIPS),
        out_specs=(VMEM, VMEM),
        scratch_shapes=[
            pltpu.VMEM((B, CHIPS * W), bf16),
            pltpu.VMEM((B, 2 * W), bf16),
            pltpu.VMEM((2 * W, CHIPS * W), bf16),
        ],
        compiler_params=PARAMS,
        cost_estimate=pl.CostEstimate(flops=2**31, bytes_accessed=2**23, transcendentals=0),
    )(at, own, other, *pieces)


def blend_kernel(core_ref, base_ref, keep_ref, got_ref, out_ref):
    out_ref[0] = base_ref[0] + 0.1 * (keep_ref[:B, :] + got_ref[:B, :])
    core = core_ref[0]
    for chip in range(CHIPS):
        rows = slice(B + chip * W, B + (chip + 1) * W)
        for part_ref, parity in ((keep_ref, core), (got_ref, 1 - core)):
            to = pl.ds(pl.multiple_of((2 * chip + parity) * W, W), W)
            out_ref[1, to, :] = base_ref[1, to, :] + 0.1 * part_ref[rows, :]


def blend(core, base, keep, got):
    return pl.pallas_call(
        blend_kernel,
        out_shape=jax.ShapeDtypeStruct(base.shape, f32),
        in_specs=[SMEM, VMEM, VMEM, VMEM],
        out_specs=VMEM,
        compiler_params=PARAMS,
    )(core, base, keep, got)


def ring(value, direction):
    pairs = [
        (x * 2 + core, (x + direction * (1 - 2 * core)) % 4 * 2 + core)
        for x in range(4)
        for core in range(2)
    ]
    return lax.ppermute(value, ("x", "core"), pairs)


def swap(value, axis):
    return lax.ppermute(value, axis, [(0, 1), (1, 0)])


def shards(grad, owner, codes, scale_ids, scale_table):
    rows_here, width_here = grad.shape
    slots = lax.axis_size("tensor")
    y, x, core = (lax.axis_index(name) for name in ("y", "x", "core"))
    chunks = grad.reshape(slots, rows_here // slots, width_here)
    spread = lax.all_to_all(chunks, "tensor", 0, 0, tiled=True)
    placed = place(spread, owner, lax.axis_index("c").reshape(1))
    own = lax.all_to_all(placed, "tensor", 0, 0, tiled=True).reshape(rows_here, width_here)
    base = dequant(scale_table, codes, scale_ids)

    behind = ring(own, 1)
    across = swap(own, "y")
    ahead = ring(own, -1)
    other = swap(own, "core")
    behind, ahead, across = lax.optimization_barrier((behind, ahead, across))
    across_ahead = ring(across, -1)
    far = ring(behind, 1)
    across_behind = swap(behind, "y")
    across_far = ring(across_ahead, -1)
    pieces = [own, behind, ahead, far, across, across_behind, across_ahead, across_far]

    step = 1 - 2 * core
    xs = [x, x - step, x + step, x + 2]
    chip = [y * 4 + at % 4 for at in xs] + [(1 - y) * 4 + at % 4 for at in xs]
    at = jnp.stack(
        [(chip[0] * 2 + core) * W, (chip[0] * 2 + 1 - core) * W] + [B + at * W for at in chip]
    ).astype(jnp.int32)
    keep, send = grams(at, own, other, pieces)
    return blend(core.reshape(1), base, keep, swap(send, "core"))


def solution(mesh):
    fine = Mesh(mesh.devices.reshape(4, 2, 4, 2, 8), ("c", "y", "x", "core", "tensor"))
    fsdp = ("c", "y", "x", "core")
    in_specs = (P("tensor", fsdp), P(), P(None, "tensor", fsdp), P(None, "tensor", fsdp), P())
    out_specs = P(None, "tensor", fsdp)
    return jax.shard_map(shards, mesh=fine, in_specs=in_specs, out_specs=out_specs, check_vma=False)
```

time: 144 us -> 110 us (0.76)
  waiting for transfers between devices: 72 us -> 43.8 us
  starting transfers between devices: 11 us -> 36.9 us
  between operations: 13.5 us -> 0.23 us
  local copies, waits for them, and re-layouts: 13.1 us -> 0.79 us
  matrix products: 8.3 us -> 0 us
  Pallas kernels: 1.89 us -> 8.09 us
  other arithmetic: 1.86 us -> 0 us
  blocking collectives: 21.9 us -> 20.1 us
    all_gather x1 -> x0, waiting for transfers between devices: 54.1 us -> none  [shards(): pieces = lax.all_gather(own, PLANE, axis=0)]
    ppermute x0 -> x9, starting transfers between devices: none -> 26 us  [the longest x5 14.1 us: ring(): return lax.ppermute(value, ('x', 'core'), pairs)]
    ppermute x0 -> x9, waiting for transfers between devices: none -> 25.9 us  [the longest x4 15.3 us: swap(): return lax.ppermute(value, axis, [(0, 1), (1, 0)])]
    all_gather x1 -> x0, local copies, waits for them, and re-layouts: 12.3 us -> none  [shards(): pieces = lax.all_gather(own, PLANE, axis=0)]
    dot_general x2 -> x0, matrix products: 8.3 us -> none  [the longest x1 5.91 us: shards(): jnp.einsum('nkc,kd->ncd', pieces, own, preferred_element_type=jnp.float32)]
    pallas_call x0 -> x3, Pallas kernels: none -> 7.49 us  [the longest x1 4.98 us: grams(): pl.pallas_call(gram_kernel, out_shape=(out, out), in_specs=[SMEM] + [VMEM...]
    add x1 -> x0, other arithmetic: 1.73 us -> none  [shards(): return 0.9 * previous.reshape(2, rows_here, width_here) + 0.1 * stacked]
    all_to_all x1, blocking collectives: 21.9 us -> 20.1 us  [shards(): lax.all_to_all(placed, 'tensor', 0, 0, tiled=True)]
  transfers between devices with their start and end apart: 2 -> 10, of which waited for: 2 -> 7; matrix products, arithmetic and copies ran while one was open for 0% -> 0% of each run, Pallas kernels for 0% -> 1%
where the time goes in v2:
time: 110 us
  waiting for transfers between devices  43.8 us (40%)
  starting transfers between devices  36.9 us (34%)
  blocking collectives  20.1 us (18%)
  Pallas kernels  8.09 us (7%)
    all_to_all x1, blocking collectives, shards(): lax.all_to_all(placed, 'tensor', 0, 0, tiled=True)  20.1 us
    all_to_all x1, waiting for transfers between devices, shards(): spread = lax.all_to_all(chunks, 'tensor', 0, 0, tiled=True)  18 us
    ppermute x4, waiting for transfers between devices, swap(): return lax.ppermute(value, axis, [(0, 1), (1, 0)])  15.3 us
    ppermute x5, starting transfers between devices, ring(): return lax.ppermute(value, ('x', 'core'), pairs)  14.1 us
    ppermute x4, starting transfers between devices, swap(): return lax.ppermute(value, axis, [(0, 1), (1, 0)])  11.9 us
    all_to_all x1, starting transfers between devices, shards(): spread = lax.all_to_all(chunks, 'tensor', 0, 0, tiled=True)  10.9 us
    ppermute x5, waiting for transfers between devices, ring(): return lax.ppermute(value, ('x', 'core'), pairs)  10.6 us
    pallas_call x1, Pallas kernels, grams(): pl.pallas_call(gram_kernel, out_shape=(out, out), in_specs=[SMEM] + [VMEM...  4.98 us
  transfers between devices with their start and end apart: 10, of which 7 were waited for; matrix products, arithmetic and copies ran while one was open for 0% of the time, Pallas kernels for 1%

profile of v2, /device:TPU:1, one launch (start us, length us, event | category | flops | bytes accessed | tf_op | source)
XLA Modules:
  0.0 109.9 jit_solution(14605506038012396198)
XLA Ops:
  0.0 10.9 %all-to-all-start = ((bf16[8,256,128]{2,1,0:T(8,128)(2,1)}), bf16[8,256,128]{2,1,0:T(8,128)(2,1)S(1)}, u32[]{:S(2)}, u32[]{:S(2)}) async-start(bf16[8,256,128]{2,1,0:T(8,128)(2,1)} %bitcast.20), calls=%async_computation | async-start | bytes 1048576 | tf_op jit(solution)/shard_map/all_to_all | solution.py:149
  10.9 18.0 %all-to-all-done.in_ref = bf16[8,256,128]{2,1,0:T(8,128)(2,1)S(1)} async-done(((bf16[8,256,128]{2,1,0:T(8,128)(2,1)}), bf16[8,256,128]{2,1,0:T(8,128)(2,1)S(1)}, u32[]{:S(2)}, u32[]{:S(2)}) %all-to-all-start) | async-done | bytes 524320 | tf_op jit(solution)/shard_map/all_to_all | solution.py:149
  28.8 0.0 copy-start.2
  28.8 0.7 copy-done.2
  29.5 0.6 shard_map.56
  30.1 20.1 %all_to_all.10 = bf16[8,256,128]{2,1,0:T(8,128)(2,1)S(1)} all-to-all(bf16[8,256,128]{2,1,0:T(8,128)(2,1)S(1)} %shard_map.56), channel_id=1, replica_groups=mesh['c'=4,'y'=2,'x'=4,'core'=2,'tensor'=8] {'tensor'}, dimensions={0} | all-to-all | bytes 1048576 | tf_op jit(solution)/shard_map/all_to_all | solution.py:151
  50.2 3.2 %collective-permute-start.3 = (bf16[2048,128]{1,0:T(8,128)(2,1)S(1)}, bf16[2048,128]{1,0:T(8,128)(2,1)S(1)}, u32[]{:S(2)}, u32[]{:S(2)}) collective-permute-start(bf16[2048,128]{1,0:T(8,128)(2,1)S(1)} %bitcast.14), channel_id=1, source_target_pairs={{0,64},{64,0},{1,65},{65,1},{2,66},{66,2},{3,67},{67,3},{4,68},{68... | collective-permute-start | bytes 1572872 | tf_op jit(solution)/shard_map/ppermute | solution.py:141
  53.4 3.1 %collective-permute-start.2 = (bf16[2048,128]{1,0:T(8,128)(2,1)S(1)}, bf16[2048,128]{1,0:T(8,128)(2,1)S(1)}, u32[]{:S(2)}, u32[]{:S(2)}) collective-permute-start(bf16[2048,128]{1,0:T(8,128)(2,1)S(1)} %bitcast.15), channel_id=1, source_target_pairs={{0,48},{8,24},{16,0},{24,40},{32,16},{40,56},{48,32},{56,8},{1,49}... | collective-permute-start | bytes 1572872 | tf_op jit(solution)/shard_map/ppermute | solution.py:137
  56.6 3.4 %collective-permute-start.1 = (bf16[2048,128]{1,0:T(8,128)(2,1)S(1)}, bf16[2048,128]{1,0:T(8,128)(2,1)S(1)}, u32[]{:S(2)}, u32[]{:S(2)}) collective-permute-start(bf16[2048,128]{1,0:T(8,128)(2,1)S(1)} %bitcast.16), channel_id=1, source_target_pairs={{0,16},{8,56},{16,32},{24,8},{32,48},{40,24},{48,0},{56,40},{1,17}... | collective-permute-start | bytes 1572872 | tf_op jit(solution)/shard_map/ppermute | solution.py:137
  60.0 4.9 %collective-permute-done.3.refs_4_ = bf16[2048,128]{1,0:T(8,128)(2,1)S(1)} collective-permute-done((bf16[2048,128]{1,0:T(8,128)(2,1)S(1)}, bf16[2048,128]{1,0:T(8,128)(2,1)S(1)}, u32[]{:S(2)}, u32[]{:S(2)}) %collective-permute-start.3) | collective-permute-done | bytes 524320 | tf_op jit(solution)/shard_map/ppermute | solution.py:141
  64.9 0.0 collective-permute-done.2.refs_2_
  64.9 6.2 %collective-permute-done.1.refs_1_ = bf16[2048,128]{1,0:T(8,128)(2,1)S(1)} collective-permute-done((bf16[2048,128]{1,0:T(8,128)(2,1)S(1)}, bf16[2048,128]{1,0:T(8,128)(2,1)S(1)}, u32[]{:S(2)}, u32[]{:S(2)}) %collective-permute-start.1) | collective-permute-done | bytes 524320 | tf_op jit(solution)/shard_map/ppermute | solution.py:137
  71.0 2.5 %collective-permute-start.6 = (bf16[2048,128]{1,0:T(8,128)(2,1)S(1)}, bf16[2048,128]{1,0:T(8,128)(2,1)S(1)}, u32[]{:S(2)}, u32[]{:S(2)}) collective-permute-start(bf16[2048,128]{1,0:T(8,128)(2,1)S(1)} %collective-permute-done.3.refs_4_), channel_id=1, source_target_pairs={{0,48},{8,24},{16,0},{24,40},{32,16},{40,56},{48,32},{56,8},{1,49}... | collective-permute-start | bytes 1572872 | tf_op jit(solution)/shard_map/ppermute | solution.py:137
  73.6 4.8 %collective-permute-start = (bf16[2048,128]{1,0:T(8,128)(2,1)S(1)}, bf16[2048,128]{1,0:T(8,128)(2,1)S(1)}, u32[]{:S(2)}, u32[]{:S(2)}) collective-permute-start(bf16[2048,128]{1,0:T(8,128)(2,1)S(1)} %bitcast.17), channel_id=1, source_target_pairs={{0,8},{8,0},{1,9},{9,1},{2,10},{10,2},{3,11},{11,3},{4,12},{12,4},... | collective-permute-start | bytes 1572872 | tf_op jit(solution)/shard_map/ppermute | solution.py:141
  78.3 2.1 %collective-permute-start.5 = (bf16[2048,128]{1,0:T(8,128)(2,1)S(1)}, bf16[2048,128]{1,0:T(8,128)(2,1)}, u32[]{:S(2)}, u32[]{:S(2)}) collective-permute-start(bf16[2048,128]{1,0:T(8,128)(2,1)S(1)} %collective-permute-done.1.refs_1_), channel_id=1, source_target_pairs={{0,64},{64,0},{1,65},{65,1},{2,66},{66,2},{3,67},{67,3},{4,68},{68... | collective-permute-start | bytes 1572872 | tf_op jit(solution)/shard_map/ppermute | solution.py:141
  80.4 1.9 %collective-permute-start.4 = (bf16[2048,128]{1,0:T(8,128)(2,1)S(1)}, bf16[2048,128]{1,0:T(8,128)(2,1)}, u32[]{:S(2)}, u32[]{:S(2)}) collective-permute-start(bf16[2048,128]{1,0:T(8,128)(2,1)S(1)} %collective-permute-done.1.refs_1_), channel_id=1, source_target_pairs={{0,16},{8,56},{16,32},{24,8},{32,48},{40,24},{48,0},{56,40},{1,17}... | collective-permute-start | bytes 1572872 | tf_op jit(solution)/shard_map/ppermute | solution.py:137
  82.4 0.3 collective-permute-done.6.refs_6_
  82.6 3.1 %collective-permute-start.7 = (bf16[2048,128]{1,0:T(8,128)(2,1)S(1)}, bf16[2048,128]{1,0:T(8,128)(2,1)}, u32[]{:S(2)}, u32[]{:S(2)}) collective-permute-start(bf16[2048,128]{1,0:T(8,128)(2,1)S(1)} %collective-permute-done.6.refs_6_), channel_id=1, source_target_pairs={{0,48},{8,24},{16,0},{24,40},{32,16},{40,56},{48,32},{56,8},{1,49}... | collective-permute-start | bytes 1572872 | tf_op jit(solution)/shard_map/ppermute | solution.py:137
  85.8 0.1 stack.43.at_ref
  85.9 0.0 copy-start
  85.9 0.0 copy-start.1
  85.9 0.0 copy-start.3
  85.9 0.0 collective-permute-done.other_ref
  85.9 7.9 %collective-permute-done.5.refs_5_ = bf16[2048,128]{1,0:T(8,128)(2,1)} collective-permute-done((bf16[2048,128]{1,0:T(8,128)(2,1)S(1)}, bf16[2048,128]{1,0:T(8,128)(2,1)}, u32[]{:S(2)}, u32[]{:S(2)}) %collective-permute-start.5) | collective-permute-done | bytes 524320 | tf_op jit(solution)/shard_map/ppermute | solution.py:141
  93.9 0.0 collective-permute-done.4.refs_3_
  93.9 4.2 %collective-permute-done.7.refs_7_ = bf16[2048,128]{1,0:T(8,128)(2,1)} collective-permute-done((bf16[2048,128]{1,0:T(8,128)(2,1)S(1)}, bf16[2048,128]{1,0:T(8,128)(2,1)}, u32[]{:S(2)}, u32[]{:S(2)}) %collective-permute-start.7) | collective-permute-done | bytes 524320 | tf_op jit(solution)/shard_map/ppermute | solution.py:137
  98.0 5.0 %shard_map.57 = (f32[3072,128]{1,0:T(8,128)S(1)}, f32[3072,128]{1,0:T(8,128)S(1)}) custom-call(s32[10]{0:T(128)S(1)} %stack.43.at_ref, bf16[2048,128]{1,0:T(8,128)(2,1)S(1)} %bitcast.18, bf16[2048,128]{1,0:T(8,128)(2,1)S(1)} %collective-permute-done.other_ref, bf16[2048,128]{1,0:T(8,128)(2,1)S(1)} %bitcast.19, ...), custom_call_target="tpu_custom_call" | custom-call | flops 2147483648 | bytes 8388608 | tf_op jit(solution)/shard_map/pallas_call | solution.py:96
  103.0 1.9 %collective-permute-start.8 = (f32[3072,128]{1,0:T(8,128)S(1)}, f32[3072,128]{1,0:T(8,128)S(1)}, u32[]{:S(2)}, u32[]{:S(2)}) collective-permute-start(f32[3072,128]{1,0:T(8,128)S(1)} %get-tuple-element.14), channel_id=1, source_target_pairs={{0,8},{8,0},{1,9},{9,1},{2,10},{10,2},{3,11},{11,3},{4,12},{12,4},... | collective-permute-start | bytes 4718600 | tf_op jit(solution)/shard_map/ppermute | solution.py:141
  105.0 0.0 copy-done
  105.0 0.0 copy-done.1
  105.0 0.0 copy-done.3
  105.0 0.9 shard_map.55.base_ref
  105.9 2.4 %collective-permute-done.8.got_ref = f32[3072,128]{1,0:T(8,128)S(1)} collective-permute-done((f32[3072,128]{1,0:T(8,128)S(1)}, f32[3072,128]{1,0:T(8,128)S(1)}, u32[]{:S(2)}, u32[]{:S(2)}) %collective-permute-start.8) | collective-permute-done | bytes 1572896 | tf_op jit(solution)/shard_map/ppermute | solution.py:141
  108.3 1.6 %shard_map.58 = f32[2,2048,128]{2,1,0:T(8,128)} custom-call(s32[1]{0:T(128)} %bitcast.core_ref, f32[2,2048,128]{2,1,0:T(8,128)S(1)} %shard_map.55.base_ref, f32[3072,128]{1,0:T(8,128)S(1)} %get-tuple-element.13.keep_ref, f32[3072,128]{1,0:T(8,128)S(1)} %collective-permute-done.8.got_ref), custom_call_target="tpu_custom_call" | custom-call | tf_op jit(solution)/shard_map/pallas_call | solution.py:122
Async XLA Ops:
  0.0 28.8 %all-to-all-start = ((bf16[8,256,128]{2,1,0:T(8,128)(2,1)}), bf16[8,256,128]{2,1,0:T(8,128)(2,1)S(1)}, u32[]{:S(2)}, u32[]{:S(2)}) async-start(bf16[8,256,128]{2,1,0:T(8,128)(2,1)} %bitcast.20), calls=%async_computation | async-start | bytes 1048576 | tf_op jit(solution)/shard_map/all_to_all | solution.py:149
  28.8 0.7 copy-start.2
  50.2 14.6 %collective-permute-start.3 = (bf16[2048,128]{1,0:T(8,128)(2,1)S(1)}, bf16[2048,128]{1,0:T(8,128)(2,1)S(1)}, u32[]{:S(2)}, u32[]{:S(2)}) collective-permute-start(bf16[2048,128]{1,0:T(8,128)(2,1)S(1)} %bitcast.14), channel_id=1, source_target_pairs={{0,64},{64,0},{1,65},{65,1},{2,66},{66,2},{3,67},{67,3},{4,68},{68... | collective-permute-start | bytes 1572872 | tf_op jit(solution)/shard_map/ppermute | solution.py:141
  53.4 11.4 %collective-permute-start.2 = (bf16[2048,128]{1,0:T(8,128)(2,1)S(1)}, bf16[2048,128]{1,0:T(8,128)(2,1)S(1)}, u32[]{:S(2)}, u32[]{:S(2)}) collective-permute-start(bf16[2048,128]{1,0:T(8,128)(2,1)S(1)} %bitcast.15), channel_id=1, source_target_pairs={{0,48},{8,24},{16,0},{24,40},{32,16},{40,56},{48,32},{56,8},{1,49}... | collective-permute-start | bytes 1572872 | tf_op jit(solution)/shard_map/ppermute | solution.py:137
  56.6 14.5 %collective-permute-start.1 = (bf16[2048,128]{1,0:T(8,128)(2,1)S(1)}, bf16[2048,128]{1,0:T(8,128)(2,1)S(1)}, u32[]{:S(2)}, u32[]{:S(2)}) collective-permute-start(bf16[2048,128]{1,0:T(8,128)(2,1)S(1)} %bitcast.16), channel_id=1, source_target_pairs={{0,16},{8,56},{16,32},{24,8},{32,48},{40,24},{48,0},{56,40},{1,17}... | collective-permute-start | bytes 1572872 | tf_op jit(solution)/shard_map/ppermute | solution.py:137
  71.0 11.6 %collective-permute-start.6 = (bf16[2048,128]{1,0:T(8,128)(2,1)S(1)}, bf16[2048,128]{1,0:T(8,128)(2,1)S(1)}, u32[]{:S(2)}, u32[]{:S(2)}) collective-permute-start(bf16[2048,128]{1,0:T(8,128)(2,1)S(1)} %collective-permute-done.3.refs_4_), channel_id=1, source_target_pairs={{0,48},{8,24},{16,0},{24,40},{32,16},{40,56},{48,32},{56,8},{1,49}... | collective-permute-start | bytes 1572872 | tf_op jit(solution)/shard_map/ppermute | solution.py:137
  73.6 12.4 %collective-permute-start = (bf16[2048,128]{1,0:T(8,128)(2,1)S(1)}, bf16[2048,128]{1,0:T(8,128)(2,1)S(1)}, u32[]{:S(2)}, u32[]{:S(2)}) collective-permute-start(bf16[2048,128]{1,0:T(8,128)(2,1)S(1)} %bitcast.17), channel_id=1, source_target_pairs={{0,8},{8,0},{1,9},{9,1},{2,10},{10,2},{3,11},{11,3},{4,12},{12,4},... | collective-permute-start | bytes 1572872 | tf_op jit(solution)/shard_map/ppermute | solution.py:141
  78.3 15.5 %collective-permute-start.5 = (bf16[2048,128]{1,0:T(8,128)(2,1)S(1)}, bf16[2048,128]{1,0:T(8,128)(2,1)}, u32[]{:S(2)}, u32[]{:S(2)}) collective-permute-start(bf16[2048,128]{1,0:T(8,128)(2,1)S(1)} %collective-permute-done.1.refs_1_), channel_id=1, source_target_pairs={{0,64},{64,0},{1,65},{65,1},{2,66},{66,2},{3,67},{67,3},{4,68},{68... | collective-permute-start | bytes 1572872 | tf_op jit(solution)/shard_map/ppermute | solution.py:141
  80.4 13.5 %collective-permute-start.4 = (bf16[2048,128]{1,0:T(8,128)(2,1)S(1)}, bf16[2048,128]{1,0:T(8,128)(2,1)}, u32[]{:S(2)}, u32[]{:S(2)}) collective-permute-start(bf16[2048,128]{1,0:T(8,128)(2,1)S(1)} %collective-permute-done.1.refs_1_), channel_id=1, source_target_pairs={{0,16},{8,56},{16,32},{24,8},{32,48},{40,24},{48,0},{56,40},{1,17}... | collective-permute-start | bytes 1572872 | tf_op jit(solution)/shard_map/ppermute | solution.py:137
  82.6 15.4 %collective-permute-start.7 = (bf16[2048,128]{1,0:T(8,128)(2,1)S(1)}, bf16[2048,128]{1,0:T(8,128)(2,1)}, u32[]{:S(2)}, u32[]{:S(2)}) collective-permute-start(bf16[2048,128]{1,0:T(8,128)(2,1)S(1)} %collective-permute-done.6.refs_6_), channel_id=1, source_target_pairs={{0,48},{8,24},{16,0},{24,40},{32,16},{40,56},{48,32},{56,8},{1,49}... | collective-permute-start | bytes 1572872 | tf_op jit(solution)/shard_map/ppermute | solution.py:137
  85.9 19.1 %copy-start = (s32[2,2048,128]{2,1,0:T(8,128)S(1)}, s32[2,2048,128]{2,1,0:T(8,128)}, u32[]{:S(2)}) copy-start(s32[2,2048,128]{2,1,0:T(8,128)} %codes_ref.1) | copy-start | bytes 6291460
  85.9 19.1 %copy-start.1 = (s32[2,16,128]{2,1,0:T(8,128)S(1)}, s32[2,16,128]{2,1,0:T(8,128)}, u32[]{:S(2)}) copy-start(s32[2,16,128]{2,1,0:T(8,128)} %ids_ref.1) | copy-start | bytes 49156
  85.9 19.1 %copy-start.3 = (f32[16]{0:T(128)S(1)}, f32[16]{0:T(128)}, u32[]{:S(2)}) copy-start(f32[16]{0:T(128)} %table_ref.1) | copy-start | bytes 196
  103.0 5.3 %collective-permute-start.8 = (f32[3072,128]{1,0:T(8,128)S(1)}, f32[3072,128]{1,0:T(8,128)S(1)}, u32[]{:S(2)}, u32[]{:S(2)}) collective-permute-start(f32[3072,128]{1,0:T(8,128)S(1)} %get-tuple-element.14), channel_id=1, source_target_pairs={{0,8},{8,0},{1,9},{9,1},{2,10},{10,2},{3,11},{11,3},{4,12},{12,4},... | collective-permute-start | bytes 4718600 | tf_op jit(solution)/shard_map/ppermute | solution.py:141

commit v3 on v2

v3 whole, which is shorter than its diff:
```python
import functools

import jax
import jax.numpy as jnp
from jax import lax
from jax.experimental import pallas as pl
from jax.experimental.pallas import tpu as pltpu
from jax.sharding import Mesh
from jax.sharding import PartitionSpec as P

B = 2048
W = 128
FIRST, SECOND = 4, 3
DEQ = 2**36
STRIP = 512
VMEM = pl.BlockSpec(memory_space=pltpu.VMEM)
SMEM = pl.BlockSpec(memory_space=pltpu.SMEM)
PARAMS = pltpu.CompilerParams(vmem_limit_bytes=40 * 2**20)
f32 = jnp.float32
bf16 = jnp.bfloat16


def place_kernel(owner_ref, block_ref, in_ref, out_ref):
    column_block = block_ref[0]
    for row_block in range(in_ref.shape[0]):
        slot = owner_ref[column_block, row_block]
        out_ref[pl.ds(slot, 1)] = in_ref[row_block : row_block + 1]


def place(chunks, owner, column_block):
    return pl.pallas_call(
        place_kernel,
        out_shape=jax.ShapeDtypeStruct(chunks.shape, chunks.dtype),
        in_specs=[SMEM, SMEM, VMEM],
        out_specs=VMEM,
        compiler_params=PARAMS,
    )(owner, column_block, chunks)


def dequant_kernel(table_ref, codes_ref, ids_ref, out_ref):
    ids = ids_ref[...]
    scale = jnp.zeros(ids.shape, f32)
    for level in range(table_ref.shape[0]):
        scale = jnp.where(ids == level, table_ref[level], scale)
    group_rows = codes_ref.shape[1] // ids.shape[1]
    for side in range(2):
        for group in range(ids.shape[1]):
            rows = slice(group * group_rows, (group + 1) * group_rows)
            code = codes_ref[side, rows, :].astype(f32)
            out_ref[side, rows, :] = 0.9 * (scale[side, group : group + 1] * ((code - 7.5) / 7.5))


def dequant(scale_table, codes, scale_ids):
    return pl.pallas_call(
        dequant_kernel,
        out_shape=jax.ShapeDtypeStruct(codes.shape, f32),
        in_specs=[SMEM, VMEM, VMEM],
        out_specs=VMEM,
        compiler_params=PARAMS,
        cost_estimate=pl.CostEstimate(flops=DEQ, bytes_accessed=2**22, transcendentals=0),
    )(scale_table, codes, scale_ids)


def left_of(block, rows, start):
    return lax.dot_general(
        block[start : start + STRIP, :],
        rows[...],
        (((1,), (1,)), ((), ())),
        preferred_element_type=f32,
    )


def right_of(piece, pair):
    return lax.dot_general(piece, pair, (((0,), (0,)), ((), ())), preferred_element_type=f32)


def collect(at_ref, pieces, block, rows):
    for i, piece in enumerate(pieces):
        block[:, i * W : (i + 1) * W] = piece[...]
    for i in range(2):
        rows[i * W : (i + 1) * W, :] = block[pl.ds(pl.multiple_of(at_ref[i], W), W), :]


def first_kernel(at_ref, *refs):
    pieces, (left_ref, block, rows) = refs[:FIRST], refs[FIRST:]
    collect(at_ref, pieces, block, rows)
    for start in range(0, B, STRIP):
        left_ref[start : start + STRIP, :] = left_of(block, rows, start)


def first_grams(at, pieces):
    return pl.pallas_call(
        first_kernel,
        out_shape=jax.ShapeDtypeStruct((B, 2 * W), f32),
        in_specs=[SMEM] + [VMEM] * FIRST,
        out_specs=VMEM,
        scratch_shapes=[pltpu.VMEM((B, FIRST * W), bf16), pltpu.VMEM((2 * W, FIRST * W), bf16)],
        compiler_params=PARAMS,
        cost_estimate=pl.CostEstimate(flops=2**30, bytes_accessed=2**22, transcendentals=0),
    )(at, *pieces)


def second_kernel(at_ref, other_ref, left_ref, *refs):
    pieces = refs[: FIRST + SECOND]
    keep_ref, send_ref, block, pair, rows = refs[FIRST + SECOND :]
    collect(at_ref, pieces[FIRST:], block, rows)
    pair[:, :W] = pieces[0][...]
    pair[:, W:] = other_ref[...]
    for start in range(0, B, STRIP):
        to = slice(start, start + STRIP)
        left = left_ref[to, :] + left_of(block, rows, start)
        keep_ref[to, :] = left[:, :W]
        send_ref[to, :] = left[:, W:]
    for i, piece in enumerate(pieces):
        to = slice(B + i * W, B + (i + 1) * W)
        right = right_of(piece[...], pair[...])
        keep_ref[to, :] = right[:, :W]
        send_ref[to, :] = right[:, W:]


def second_grams(at, other, left, pieces):
    out = jax.ShapeDtypeStruct((B + (FIRST + SECOND) * W, W), f32)
    return pl.pallas_call(
        second_kernel,
        out_shape=(out, out),
        in_specs=[SMEM] + [VMEM] * (2 + FIRST + SECOND),
        out_specs=(VMEM, VMEM),
        scratch_shapes=[
            pltpu.VMEM((B, SECOND * W), bf16),
            pltpu.VMEM((B, 2 * W), bf16),
            pltpu.VMEM((2 * W, SECOND * W), bf16),
        ],
        compiler_params=PARAMS,
        cost_estimate=pl.CostEstimate(flops=2**30, bytes_accessed=2**22, transcendentals=0),
    )(at, other, left, *pieces)


def finish_kernel(at_ref, base_ref, keep_ref, got_ref, own_ref, last_ref, got_last_ref, out_ref, block, rows):
    block[:, :W] = last_ref[...]
    block[:, W:] = got_last_ref[...]
    rows[...] = block[pl.ds(pl.multiple_of(at_ref[0], W), W), :]
    for start in range(0, B, STRIP):
        to = slice(start, start + STRIP)
        left = keep_ref[to, :] + got_ref[to, :] + left_of(block, rows, start)
        out_ref[0, to, :] = base_ref[0, to, :] + 0.1 * left
    right = right_of(block[...], own_ref[...])
    early = FIRST + SECOND
    for side, part_ref in enumerate((keep_ref, got_ref)):
        for i in range(early + 1):
            to = pl.ds(pl.multiple_of(at_ref[2 + side * (early + 1) + i], W), W)
            if i < early:
                part = part_ref[B + i * W : B + (i + 1) * W, :]
            else:
                part = right[side * W : (side + 1) * W, :]
            out_ref[1, to, :] = base_ref[1, to, :] + 0.1 * part


def finish(at, base, keep, got, own, last, got_last):
    return pl.pallas_call(
        finish_kernel,
        out_shape=jax.ShapeDtypeStruct(base.shape, f32),
        in_specs=[SMEM] + [VMEM] * 6,
        out_specs=VMEM,
        scratch_shapes=[pltpu.VMEM((B, 2 * W), bf16), pltpu.VMEM((W, 2 * W), bf16)],
        compiler_params=PARAMS,
    )(at, base, keep, got, own, last, got_last)


def ring(value, direction):
    pairs = [
        (x * 2 + core, (x + direction * (1 - 2 * core)) % 4 * 2 + core)
        for x in range(4)
        for core in range(2)
    ]
    return lax.ppermute(value, ("x", "core"), pairs)


def swap(value, axis):
    return lax.ppermute(value, axis, [(0, 1), (1, 0)])


def shards(grad, owner, codes, scale_ids, scale_table):
    rows_here, width_here = grad.shape
    slots = lax.axis_size("tensor")
    y, x, core = (lax.axis_index(name) for name in ("y", "x", "core"))
    chunks = grad.reshape(slots, rows_here // slots, width_here)
    spread = lax.all_to_all(chunks, "tensor", 0, 0, tiled=True)
    placed = place(spread, owner, lax.axis_index("c").reshape(1))
    own = lax.all_to_all(placed, "tensor", 0, 0, tiled=True).reshape(rows_here, width_here)
    base = dequant(scale_table, codes, scale_ids)

    def row_starts(core):
        step = 1 - 2 * core
        xs = [x, x - step, x + step, x, x + 2, x - step, x + step, x + 2]
        ys = [y, y, y, 1 - y, y, 1 - y, 1 - y, 1 - y]
        return [((row * 4 + column % 4) * 2 + core) * W for row, column in zip(ys, xs)]

    mine, theirs = row_starts(core), row_starts(1 - core)
    at = jnp.stack([mine[0], theirs[0]] + mine + theirs).astype(jnp.int32)
    across = swap(own, "y")
    behind = ring(own, 1)
    ahead = ring(own, -1)
    across_behind = swap(behind, "y")
    other = swap(lax.optimization_barrier((own, behind))[0], "core")
    ahead, other = lax.optimization_barrier((ahead, other))
    across_ahead = ring(across, -1)
    far = ring(ahead, -1)
    left = first_grams(at, [own, behind, ahead, across])
    left, across_ahead = lax.optimization_barrier((left, across_ahead))
    across_far = ring(across_ahead, -1)
    pieces = [own, behind, ahead, across, far, across_behind, across_ahead]
    keep, send = second_grams(at, other, left, pieces)
    got, got_far = swap(send, "core"), swap(across_far, "core")
    return finish(at, base, keep, got, own, across_far, got_far)


def solution(mesh):
    fine = Mesh(mesh.devices.reshape(4, 2, 4, 2, 8), ("c", "y", "x", "core", "tensor"))
    fsdp = ("c", "y", "x", "core")
    in_specs = (P("tensor", fsdp), P(), P(None, "tensor", fsdp), P(None, "tensor", fsdp), P())
    out_specs = P(None, "tensor", fsdp)
    return jax.shard_map(shards, mesh=fine, in_specs=in_specs, out_specs=out_specs, check_vma=False)
```

time: 110 us -> 101 us (0.918)
  waiting for transfers between devices: 43.8 us -> 30.5 us
  starting transfers between devices: 36.9 us -> 39.9 us
    ppermute x5, waiting for transfers between devices: 10.6 us -> 3.83 us  [ring(): return lax.ppermute(value, ('x', 'core'), pairs)]
    ppermute x4 -> x5, waiting for transfers between devices: 15.3 us -> 8.69 us  [swap(): return lax.ppermute(value, axis, [(0, 1), (1, 0)])]
    ppermute x4 -> x5, starting transfers between devices: 11.9 us -> 17 us  [swap(): return lax.ppermute(value, axis, [(0, 1), (1, 0)])]
    ppermute x5, starting transfers between devices: 14.1 us -> 12 us  [ring(): return lax.ppermute(value, ('x', 'core'), pairs)]
    pallas_call x2 -> x3, Pallas kernels: 6.59 us -> 7.18 us  [the longest x1 2.87 us: finish(): pl.pallas_call(finish_kernel, out_shape=jax.ShapeDtypeStruct(base.shape,...]
  transfers between devices with their start and end apart: 10 -> 11, of which waited for: 7 -> 7; matrix products, arithmetic and copies ran while one was open for 0% -> 0% of each run, Pallas kernels for 1% -> 5%
where the time goes in v3:
time: 101 us; the launch traced here: 100 us
  starting transfers between devices  39.9 us (40%)
  waiting for transfers between devices  30.5 us (30%)
  blocking collectives  20.1 us (20%)
  Pallas kernels  8.68 us (9%)
    all_to_all x1, blocking collectives, shards(): lax.all_to_all(placed, 'tensor', 0, 0, tiled=True)  20.1 us
    all_to_all x1, waiting for transfers between devices, shards(): spread = lax.all_to_all(chunks, 'tensor', 0, 0, tiled=True)  18 us
    ppermute x5, starting transfers between devices, swap(): return lax.ppermute(value, axis, [(0, 1), (1, 0)])  17 us
    ppermute x5, starting transfers between devices, ring(): return lax.ppermute(value, ('x', 'core'), pairs)  12 us
    all_to_all x1, starting transfers between devices, shards(): spread = lax.all_to_all(chunks, 'tensor', 0, 0, tiled=True)  10.9 us
    ppermute x5, waiting for transfers between devices, swap(): return lax.ppermute(value, axis, [(0, 1), (1, 0)])  8.69 us
    ppermute x5, waiting for transfers between devices, ring(): return lax.ppermute(value, ('x', 'core'), pairs)  3.83 us
    pallas_call x1, Pallas kernels, finish(): pl.pallas_call(finish_kernel, out_shape=jax.ShapeDtypeStruct(base.shape,...  2.87 us
  transfers between devices with their start and end apart: 11, of which 7 were waited for; matrix products, arithmetic and copies ran while one was open for 0% of the time, Pallas kernels for 5%

profile of v3, /device:TPU:1, one launch (start us, length us, event | category | flops | bytes accessed | tf_op | source)
XLA Modules:
  0.0 100.3 jit_solution(10163256202117884400)
XLA Ops:
  0.0 10.9 %all-to-all-start = ((bf16[8,256,128]{2,1,0:T(8,128)(2,1)}), bf16[8,256,128]{2,1,0:T(8,128)(2,1)S(1)}, u32[]{:S(2)}, u32[]{:S(2)}) async-start(bf16[8,256,128]{2,1,0:T(8,128)(2,1)} %bitcast.26), calls=%async_computation | async-start | bytes 1048576 | tf_op jit(solution)/shard_map/all_to_all | solution.py:187
  10.9 18.0 %all-to-all-done.in_ref = bf16[8,256,128]{2,1,0:T(8,128)(2,1)S(1)} async-done(((bf16[8,256,128]{2,1,0:T(8,128)(2,1)}), bf16[8,256,128]{2,1,0:T(8,128)(2,1)S(1)}, u32[]{:S(2)}, u32[]{:S(2)}) %all-to-all-start) | async-done | bytes 524320 | tf_op jit(solution)/shard_map/all_to_all | solution.py:187
  28.8 0.0 copy-start
  28.8 0.7 copy-done
  29.5 0.6 shard_map.56
  30.1 20.1 %all_to_all.10 = bf16[8,256,128]{2,1,0:T(8,128)(2,1)S(1)} all-to-all(bf16[8,256,128]{2,1,0:T(8,128)(2,1)S(1)} %shard_map.56), channel_id=1, replica_groups=mesh['c'=4,'y'=2,'x'=4,'core'=2,'tensor'=8] {'tensor'}, dimensions={0} | all-to-all | bytes 1048576 | tf_op jit(solution)/shard_map/all_to_all | solution.py:189
  50.2 4.4 %collective-permute-start.1 = (bf16[2048,128]{1,0:T(8,128)(2,1)S(1)}, bf16[2048,128]{1,0:T(8,128)(2,1)S(1)}, u32[]{:S(2)}, u32[]{:S(2)}) collective-permute-start(bf16[2048,128]{1,0:T(8,128)(2,1)S(1)} %bitcast.19), channel_id=1, source_target_pairs={{0,16},{8,56},{16,32},{24,8},{32,48},{40,24},{48,0},{56,40},{1,17}... | collective-permute-start | bytes 1572872 | tf_op jit(solution)/shard_map/ppermute | solution.py:175
  54.6 3.2 %collective-permute-start.3 = (bf16[2048,128]{1,0:T(8,128)(2,1)S(1)}, bf16[2048,128]{1,0:T(8,128)(2,1)S(1)}, u32[]{:S(2)}, u32[]{:S(2)}) collective-permute-start(bf16[2048,128]{1,0:T(8,128)(2,1)S(1)} %bitcast.20), channel_id=1, source_target_pairs={{0,64},{64,0},{1,65},{65,1},{2,66},{66,2},{3,67},{67,3},{4,68},{68... | collective-permute-start | bytes 1572872 | tf_op jit(solution)/shard_map/ppermute | solution.py:179
  57.8 1.9 %collective-permute-start = (bf16[2048,128]{1,0:T(8,128)(2,1)S(1)}, bf16[2048,128]{1,0:T(8,128)(2,1)S(1)}, u32[]{:S(2)}, u32[]{:S(2)}) collective-permute-start(bf16[2048,128]{1,0:T(8,128)(2,1)S(1)} %bitcast.21), channel_id=1, source_target_pairs={{0,48},{8,24},{16,0},{24,40},{32,16},{40,56},{48,32},{56,8},{1,49}... | collective-permute-start | bytes 1572872 | tf_op jit(solution)/shard_map/ppermute | solution.py:175
  59.8 1.0 collective-permute-done.1.refs_1_
  60.7 4.4 %collective-permute-start.2 = (bf16[2048,128]{1,0:T(8,128)(2,1)S(1)}, bf16[2048,128]{1,0:T(8,128)(2,1)S(1)}, u32[]{:S(2)}, u32[]{:S(2)}) collective-permute-start(bf16[2048,128]{1,0:T(8,128)(2,1)S(1)} %bitcast.22), channel_id=1, source_target_pairs={{0,8},{8,0},{1,9},{9,1},{2,10},{10,2},{3,11},{11,3},{4,12},{12,4},... | collective-permute-start | bytes 1572872 | tf_op jit(solution)/shard_map/ppermute | solution.py:179
  65.2 5.1 %collective-permute-done.3.refs_3_ = bf16[2048,128]{1,0:T(8,128)(2,1)S(1)} collective-permute-done((bf16[2048,128]{1,0:T(8,128)(2,1)S(1)}, bf16[2048,128]{1,0:T(8,128)(2,1)S(1)}, u32[]{:S(2)}, u32[]{:S(2)}) %collective-permute-start.3) | collective-permute-done | bytes 524320 | tf_op jit(solution)/shard_map/ppermute | solution.py:179
  70.3 1.9 %collective-permute-start.4 = (bf16[2048,128]{1,0:T(8,128)(2,1)S(1)}, bf16[2048,128]{1,0:T(8,128)(2,1)S(1)}, u32[]{:S(2)}, u32[]{:S(2)}) collective-permute-start(bf16[2048,128]{1,0:T(8,128)(2,1)S(1)} %collective-permute-done.3.refs_3_), channel_id=1, source_target_pairs={{0,48},{8,24},{16,0},{24,40},{32,16},{40,56},{48,32},{56,8},{1,49}... | collective-permute-start | bytes 1572872 | tf_op jit(solution)/shard_map/ppermute | solution.py:175
  72.3 0.1 stack.69.at_ref
  72.4 3.2 %collective-permute-start.6 = (bf16[2048,128]{1,0:T(8,128)(2,1)S(1)}, bf16[2048,128]{1,0:T(8,128)(2,1)S(1)}, u32[]{:S(2)}, u32[]{:S(2)}) collective-permute-start(bf16[2048,128]{1,0:T(8,128)(2,1)S(1)} %collective-permute-done.1.refs_1_), channel_id=1, source_target_pairs={{0,64},{64,0},{1,65},{65,1},{2,66},{66,2},{3,67},{67,3},{4,68},{68... | collective-permute-start | bytes 1572872 | tf_op jit(solution)/shard_map/ppermute | solution.py:179
  75.6 0.0 collective-permute-done.refs_2_
  75.6 0.0 collective-permute-done.2.other_ref
  75.6 1.9 %collective-permute-start.5 = (bf16[2048,128]{1,0:T(8,128)(2,1)S(1)}, bf16[2048,128]{1,0:T(8,128)(2,1)S(1)}, u32[]{:S(2)}, u32[]{:S(2)}) collective-permute-start(bf16[2048,128]{1,0:T(8,128)(2,1)S(1)} %collective-permute-done.refs_2_), channel_id=1, source_target_pairs={{0,48},{8,24},{16,0},{24,40},{32,16},{40,56},{48,32},{56,8},{1,49}... | collective-permute-start | bytes 1572872 | tf_op jit(solution)/shard_map/ppermute | solution.py:175
  77.6 1.6 %shard_map.57.left_ref = f32[2048,256]{1,0:T(8,128)S(1)} custom-call(s32[18]{0:T(128)S(1)} %stack.69.at_ref, bf16[2048,128]{1,0:T(8,128)(2,1)S(1)} %bitcast.23, bf16[2048,128]{1,0:T(8,128)(2,1)S(1)} %collective-permute-done.1.refs_1_, bf16[2048,128]{1,0:T(8,128)(2,1)S(1)} %collective-permute-done.refs_2_, bf16[2048,128]{1,0:T(8,128)(2,1)S(1)} %collective-permute-done.3.refs_3_), custom_call_target="tpu_custom_call" | custom-call | flops 1073741824 | bytes 4194304 | tf_op jit(solution)/shard_map/pallas_call | solution.py:92
  79.2 0.0 copy-start.1
  79.2 0.0 copy-start.2
  79.2 0.0 copy-start.3
  79.2 2.2 %collective-permute-done.4.refs_6_ = bf16[2048,128]{1,0:T(8,128)(2,1)S(1)} collective-permute-done((bf16[2048,128]{1,0:T(8,128)(2,1)S(1)}, bf16[2048,128]{1,0:T(8,128)(2,1)S(1)}, u32[]{:S(2)}, u32[]{:S(2)}) %collective-permute-start.4) | collective-permute-done | bytes 524320 | tf_op jit(solution)/shard_map/ppermute | solution.py:175
  81.4 1.9 %collective-permute-start.8 = (bf16[2048,128]{1,0:T(8,128)(2,1)S(1)}, bf16[2048,128]{1,0:T(8,128)(2,1)S(1)}, u32[]{:S(2)}, u32[]{:S(2)}) collective-permute-start(bf16[2048,128]{1,0:T(8,128)(2,1)S(1)} %collective-permute-done.4.refs_6_), channel_id=1, source_target_pairs={{0,48},{8,24},{16,0},{24,40},{32,16},{40,56},{48,32},{56,8},{1,49}... | collective-permute-start | bytes 1572872 | tf_op jit(solution)/shard_map/ppermute | solution.py:175
  83.3 3.0 %collective-permute-done.6.refs_5_ = bf16[2048,128]{1,0:T(8,128)(2,1)S(1)} collective-permute-done((bf16[2048,128]{1,0:T(8,128)(2,1)S(1)}, bf16[2048,128]{1,0:T(8,128)(2,1)S(1)}, u32[]{:S(2)}, u32[]{:S(2)}) %collective-permute-start.6) | collective-permute-done | bytes 524320 | tf_op jit(solution)/shard_map/ppermute | solution.py:179
  86.3 0.7 collective-permute-done.5.refs_4_
  87.0 2.7 %shard_map.58 = (f32[2944,128]{1,0:T(8,128)S(1)}, f32[2944,128]{1,0:T(8,128)S(1)}) custom-call(s32[18]{0:T(128)S(1)} %stack.69.at_ref, bf16[2048,128]{1,0:T(8,128)(2,1)S(1)} %collective-permute-done.2.other_ref, f32[2048,256]{1,0:T(8,128)S(1)} %shard_map.57.left_ref, bf16[2048,128]{1,0:T(8,128)(2,1)S(1)} %bitcast.24, ...), custom_call_target="tpu_custom_call" | custom-call | flops 1073741824 | bytes 4194304 | tf_op jit(solution)/shard_map/pallas_call | solution.py:123
  89.7 3.5 %collective-permute-start.7 = (f32[2944,128]{1,0:T(8,128)S(1)}, f32[2944,128]{1,0:T(8,128)S(1)}, u32[]{:S(2)}, u32[]{:S(2)}) collective-permute-start(f32[2944,128]{1,0:T(8,128)S(1)} %get-tuple-element.18), channel_id=1, source_target_pairs={{0,8},{8,0},{1,9},{9,1},{2,10},{10,2},{3,11},{11,3},{4,12},{12,4},... | collective-permute-start | bytes 4521992 | tf_op jit(solution)/shard_map/ppermute | solution.py:179
  93.2 0.0 collective-permute-done.8.last_ref
  93.2 2.7 %collective-permute-start.9 = (bf16[2048,128]{1,0:T(8,128)(2,1)S(1)}, bf16[2048,128]{1,0:T(8,128)(2,1)S(1)}, u32[]{:S(2)}, u32[]{:S(2)}) collective-permute-start(bf16[2048,128]{1,0:T(8,128)(2,1)S(1)} %collective-permute-done.8.last_ref), channel_id=1, source_target_pairs={{0,8},{8,0},{1,9},{9,1},{2,10},{10,2},{3,11},{11,3},{4,12},{12,4},... | collective-permute-start | bytes 1572872 | tf_op jit(solution)/shard_map/ppermute | solution.py:179
  95.9 0.0 copy-done.1
  95.9 0.0 copy-done.2
  95.9 0.0 copy-done.3
  96.0 0.9 shard_map.55.base_ref
  96.9 0.6 collective-permute-done.9.got_last_ref
  97.4 0.0 collective-permute-done.7.got_ref
  97.4 2.9 %shard_map.59 = f32[2,2048,128]{2,1,0:T(8,128)} custom-call(s32[18]{0:T(128)S(1)} %stack.69.at_ref, f32[2,2048,128]{2,1,0:T(8,128)S(1)} %shard_map.55.base_ref, f32[2944,128]{1,0:T(8,128)S(1)} %get-tuple-element.17.keep_ref, f32[2944,128]{1,0:T(8,128)S(1)} %collective-permute-done.7.got_ref, bf16[2048,128]{1,0:T(8,128)(2,1)S(1)} %bitcast.25, ...), custom_call_target="tpu_custom_call" | custom-call | tf_op jit(solution)/shard_map/pallas_call | solution.py:159
Async XLA Ops:
  0.0 28.8 %all-to-all-start = ((bf16[8,256,128]{2,1,0:T(8,128)(2,1)}), bf16[8,256,128]{2,1,0:T(8,128)(2,1)S(1)}, u32[]{:S(2)}, u32[]{:S(2)}) async-start(bf16[8,256,128]{2,1,0:T(8,128)(2,1)} %bitcast.26), calls=%async_computation | async-start | bytes 1048576 | tf_op jit(solution)/shard_map/all_to_all | solution.py:187
  28.8 0.7 copy-start
  50.2 10.5 %collective-permute-start.1 = (bf16[2048,128]{1,0:T(8,128)(2,1)S(1)}, bf16[2048,128]{1,0:T(8,128)(2,1)S(1)}, u32[]{:S(2)}, u32[]{:S(2)}) collective-permute-start(bf16[2048,128]{1,0:T(8,128)(2,1)S(1)} %bitcast.19), channel_id=1, source_target_pairs={{0,16},{8,56},{16,32},{24,8},{32,48},{40,24},{48,0},{56,40},{1,17}... | collective-permute-start | bytes 1572872 | tf_op jit(solution)/shard_map/ppermute | solution.py:175
  54.6 15.6 %collective-permute-start.3 = (bf16[2048,128]{1,0:T(8,128)(2,1)S(1)}, bf16[2048,128]{1,0:T(8,128)(2,1)S(1)}, u32[]{:S(2)}, u32[]{:S(2)}) collective-permute-start(bf16[2048,128]{1,0:T(8,128)(2,1)S(1)} %bitcast.20), channel_id=1, source_target_pairs={{0,64},{64,0},{1,65},{65,1},{2,66},{66,2},{3,67},{67,3},{4,68},{68... | collective-permute-start | bytes 1572872 | tf_op jit(solution)/shard_map/ppermute | solution.py:179
  57.8 17.8 %collective-permute-start = (bf16[2048,128]{1,0:T(8,128)(2,1)S(1)}, bf16[2048,128]{1,0:T(8,128)(2,1)S(1)}, u32[]{:S(2)}, u32[]{:S(2)}) collective-permute-start(bf16[2048,128]{1,0:T(8,128)(2,1)S(1)} %bitcast.21), channel_id=1, source_target_pairs={{0,48},{8,24},{16,0},{24,40},{32,16},{40,56},{48,32},{56,8},{1,49}... | collective-permute-start | bytes 1572872 | tf_op jit(solution)/shard_map/ppermute | solution.py:175
  60.7 14.9 %collective-permute-start.2 = (bf16[2048,128]{1,0:T(8,128)(2,1)S(1)}, bf16[2048,128]{1,0:T(8,128)(2,1)S(1)}, u32[]{:S(2)}, u32[]{:S(2)}) collective-permute-start(bf16[2048,128]{1,0:T(8,128)(2,1)S(1)} %bitcast.22), channel_id=1, source_target_pairs={{0,8},{8,0},{1,9},{9,1},{2,10},{10,2},{3,11},{11,3},{4,12},{12,4},... | collective-permute-start | bytes 1572872 | tf_op jit(solution)/shard_map/ppermute | solution.py:179
  70.3 11.1 %collective-permute-start.4 = (bf16[2048,128]{1,0:T(8,128)(2,1)S(1)}, bf16[2048,128]{1,0:T(8,128)(2,1)S(1)}, u32[]{:S(2)}, u32[]{:S(2)}) collective-permute-start(bf16[2048,128]{1,0:T(8,128)(2,1)S(1)} %collective-permute-done.3.refs_3_), channel_id=1, source_target_pairs={{0,48},{8,24},{16,0},{24,40},{32,16},{40,56},{48,32},{56,8},{1,49}... | collective-permute-start | bytes 1572872 | tf_op jit(solution)/shard_map/ppermute | solution.py:175
  72.4 13.9 %collective-permute-start.6 = (bf16[2048,128]{1,0:T(8,128)(2,1)S(1)}, bf16[2048,128]{1,0:T(8,128)(2,1)S(1)}, u32[]{:S(2)}, u32[]{:S(2)}) collective-permute-start(bf16[2048,128]{1,0:T(8,128)(2,1)S(1)} %collective-permute-done.1.refs_1_), channel_id=1, source_target_pairs={{0,64},{64,0},{1,65},{65,1},{2,66},{66,2},{3,67},{67,3},{4,68},{68... | collective-permute-start | bytes 1572872 | tf_op jit(solution)/shard_map/ppermute | solution.py:179
  75.6 11.4 %collective-permute-start.5 = (bf16[2048,128]{1,0:T(8,128)(2,1)S(1)}, bf16[2048,128]{1,0:T(8,128)(2,1)S(1)}, u32[]{:S(2)}, u32[]{:S(2)}) collective-permute-start(bf16[2048,128]{1,0:T(8,128)(2,1)S(1)} %collective-permute-done.refs_2_), channel_id=1, source_target_pairs={{0,48},{8,24},{16,0},{24,40},{32,16},{40,56},{48,32},{56,8},{1,49}... | collective-permute-start | bytes 1572872 | tf_op jit(solution)/shard_map/ppermute | solution.py:175
  79.2 16.7 %copy-start.1 = (s32[2,2048,128]{2,1,0:T(8,128)S(1)}, s32[2,2048,128]{2,1,0:T(8,128)}, u32[]{:S(2)}) copy-start(s32[2,2048,128]{2,1,0:T(8,128)} %codes_ref.1) | copy-start | bytes 6291460
  79.2 16.7 %copy-start.2 = (s32[2,16,128]{2,1,0:T(8,128)S(1)}, s32[2,16,128]{2,1,0:T(8,128)}, u32[]{:S(2)}) copy-start(s32[2,16,128]{2,1,0:T(8,128)} %ids_ref.1) | copy-start | bytes 49156
  79.2 16.7 %copy-start.3 = (f32[16]{0:T(128)S(1)}, f32[16]{0:T(128)}, u32[]{:S(2)}) copy-start(f32[16]{0:T(128)} %table_ref.1) | copy-start | bytes 196
  81.4 11.8 %collective-permute-start.8 = (bf16[2048,128]{1,0:T(8,128)(2,1)S(1)}, bf16[2048,128]{1,0:T(8,128)(2,1)S(1)}, u32[]{:S(2)}, u32[]{:S(2)}) collective-permute-start(bf16[2048,128]{1,0:T(8,128)(2,1)S(1)} %collective-permute-done.4.refs_6_), channel_id=1, source_target_pairs={{0,48},{8,24},{16,0},{24,40},{32,16},{40,56},{48,32},{56,8},{1,49}... | collective-permute-start | bytes 1572872 | tf_op jit(solution)/shard_map/ppermute | solution.py:175
  89.7 7.8 %collective-permute-start.7 = (f32[2944,128]{1,0:T(8,128)S(1)}, f32[2944,128]{1,0:T(8,128)S(1)}, u32[]{:S(2)}, u32[]{:S(2)}) collective-permute-start(f32[2944,128]{1,0:T(8,128)S(1)} %get-tuple-element.18), channel_id=1, source_target_pairs={{0,8},{8,0},{1,9},{9,1},{2,10},{10,2},{3,11},{11,3},{4,12},{12,4},... | collective-permute-start | bytes 4521992 | tf_op jit(solution)/shard_map/ppermute | solution.py:179
  93.2 4.2 %collective-permute-start.9 = (bf16[2048,128]{1,0:T(8,128)(2,1)S(1)}, bf16[2048,128]{1,0:T(8,128)(2,1)S(1)}, u32[]{:S(2)}, u32[]{:S(2)}) collective-permute-start(bf16[2048,128]{1,0:T(8,128)(2,1)S(1)} %collective-permute-done.8.last_ref), channel_id=1, source_target_pairs={{0,8},{8,0},{1,9},{9,1},{2,10},{10,2},{3,11},{11,3},{4,12},{12,4},... | collective-permute-start | bytes 1572872 | tf_op jit(solution)/shard_map/ppermute | solution.py:179

commit v4 on v3

v4 whole, which is shorter than its diff:
```python
import functools

import jax
import jax.numpy as jnp
from jax import lax
from jax.experimental import pallas as pl
from jax.experimental.pallas import tpu as pltpu
from jax.sharding import Mesh
from jax.sharding import PartitionSpec as P

B = 2048
W = 128
FIRST, MIDDLE, SECOND = 4, 5, 3
STRIP = 512
WEIGHT = 2**36
VMEM = pl.BlockSpec(memory_space=pltpu.VMEM)
SMEM = pl.BlockSpec(memory_space=pltpu.SMEM)
PARAMS = pltpu.CompilerParams(vmem_limit_bytes=20 * 2**20)
f32 = jnp.float32
bf16 = jnp.bfloat16


def place_kernel(slots_ref, in_ref, out_ref):
    for row_block in range(in_ref.shape[0]):
        out_ref[pl.ds(slots_ref[row_block], 1)] = in_ref[row_block : row_block + 1]


def place(chunks, slots):
    return pl.pallas_call(
        place_kernel,
        out_shape=jax.ShapeDtypeStruct(chunks.shape, chunks.dtype),
        in_specs=[SMEM, VMEM],
        out_specs=VMEM,
        compiler_params=PARAMS,
    )(slots, chunks)


def dequant_kernel(table_ref, codes_ref, ids_ref, out_ref):
    ids = ids_ref[0]
    scale = jnp.zeros(ids.shape, f32)
    for level in range(table_ref.shape[0]):
        scale = jnp.where(ids == level, table_ref[level], scale)
    group_rows = codes_ref.shape[1] // ids.shape[0]
    for group in range(ids.shape[0]):
        rows = slice(group * group_rows, (group + 1) * group_rows)
        code = codes_ref[0, rows, :].astype(f32)
        out_ref[rows, :] = 0.9 * (scale[group : group + 1] * ((code - 7.5) / 7.5))


def dequant(side, scale_table, codes, scale_ids):
    def block(array):
        return pl.BlockSpec((1, *array.shape[1:]), lambda i: (side, 0, 0))

    return pl.pallas_call(
        dequant_kernel,
        grid=(1,),
        out_shape=jax.ShapeDtypeStruct(codes.shape[1:], f32),
        in_specs=[SMEM, block(codes), block(scale_ids)],
        out_specs=pl.BlockSpec(codes.shape[1:], lambda i: (0, 0)),
        compiler_params=PARAMS,
        cost_estimate=pl.CostEstimate(flops=WEIGHT, bytes_accessed=2**21, transcendentals=0),
    )(scale_table, codes, scale_ids)


def left_of(block, rows, start):
    return lax.dot_general(
        block[start : start + STRIP, :],
        rows[...],
        (((1,), (1,)), ((), ())),
        preferred_element_type=f32,
    )


def right_of(piece, pair):
    return lax.dot_general(piece, pair, (((0,), (0,)), ((), ())), preferred_element_type=f32)


def collect(at_ref, pieces, block, rows):
    for i, piece in enumerate(pieces):
        block[:, i * W : (i + 1) * W] = piece[...]
    for i in range(2):
        rows[i * W : (i + 1) * W, :] = block[pl.ds(pl.multiple_of(at_ref[i], W), W), :]


def first_kernel(at_ref, *refs):
    pieces, (left_ref, block, rows) = refs[:FIRST], refs[FIRST:]
    collect(at_ref, pieces, block, rows)
    for start in range(0, B, STRIP):
        left_ref[start : start + STRIP, :] = left_of(block, rows, start)


def first_grams(at, pieces):
    return pl.pallas_call(
        first_kernel,
        out_shape=jax.ShapeDtypeStruct((B, 2 * W), f32),
        in_specs=[SMEM] + [VMEM] * FIRST,
        out_specs=VMEM,
        scratch_shapes=[pltpu.VMEM((B, FIRST * W), bf16), pltpu.VMEM((2 * W, FIRST * W), bf16)],
        compiler_params=PARAMS,
        cost_estimate=pl.CostEstimate(flops=2**30, bytes_accessed=2**22, transcendentals=0),
    )(at, *pieces)


def middle_kernel(own_ref, other_ref, *refs):
    pieces, (right_ref, pair) = refs[:MIDDLE], refs[MIDDLE:]
    pair[:, :W] = own_ref[...]
    pair[:, W:] = other_ref[...]
    for i, piece in enumerate(pieces):
        right_ref[i * W : (i + 1) * W, :] = right_of(piece[...], pair[...])


def middle_grams(own, other, pieces):
    return pl.pallas_call(
        middle_kernel,
        out_shape=jax.ShapeDtypeStruct((MIDDLE * W, 2 * W), f32),
        in_specs=[VMEM] * (2 + MIDDLE),
        out_specs=VMEM,
        scratch_shapes=[pltpu.VMEM((B, 2 * W), bf16)],
        compiler_params=PARAMS,
        cost_estimate=pl.CostEstimate(flops=2**30, bytes_accessed=2**22, transcendentals=0),
    )(own, other, *pieces)


def second_kernel(at_ref, own_ref, other_ref, left_ref, right_ref, *refs):
    pieces, (keep_ref, send_ref, block, pair, rows) = refs[:SECOND], refs[SECOND:]
    collect(at_ref, pieces, block, rows)
    pair[:, :W] = own_ref[...]
    pair[:, W:] = other_ref[...]
    for start in range(0, B, STRIP):
        to = slice(start, start + STRIP)
        left = left_ref[to, :] + left_of(block, rows, start)
        keep_ref[to, :] = left[:, :W]
        send_ref[to, :] = left[:, W:]
    middle = B + MIDDLE * W
    keep_ref[B:middle, :] = right_ref[:, :W]
    send_ref[B:middle, :] = right_ref[:, W:]
    for i, piece in enumerate(pieces[MIDDLE - FIRST :]):
        to = slice(middle + i * W, middle + (i + 1) * W)
        right = right_of(piece[...], pair[...])
        keep_ref[to, :] = right[:, :W]
        send_ref[to, :] = right[:, W:]


def second_grams(at, own, other, left, right, pieces):
    out = jax.ShapeDtypeStruct((B + (FIRST + SECOND) * W, W), f32)
    return pl.pallas_call(
        second_kernel,
        out_shape=(out, out),
        in_specs=[SMEM] + [VMEM] * (4 + SECOND),
        out_specs=(VMEM, VMEM),
        scratch_shapes=[
            pltpu.VMEM((B, SECOND * W), bf16),
            pltpu.VMEM((B, 2 * W), bf16),
            pltpu.VMEM((2 * W, SECOND * W), bf16),
        ],
        compiler_params=PARAMS,
        cost_estimate=pl.CostEstimate(flops=2**30, bytes_accessed=2**22, transcendentals=0),
    )(at, own, other, left, right, *pieces)


def sum_kernel(at_ref, base_left, base_right, keep_ref, got_ref, own_ref, last_ref, left_ref, right_ref, rows):
    rows[...] = last_ref[pl.ds(pl.multiple_of(at_ref[0], W), W), :]
    for start in range(0, B, STRIP):
        to = slice(start, start + STRIP)
        left = keep_ref[to, :] + got_ref[to, :] + left_of(last_ref, rows, start)
        left_ref[to, :] = base_left[to, :] + 0.1 * left
    last = right_of(last_ref[...], own_ref[...])
    early = FIRST + SECOND
    for side, part_ref in enumerate((keep_ref, got_ref)):
        for i in range(early + 1 - side):
            to = pl.ds(pl.multiple_of(at_ref[2 + side * (early + 1) + i], W), W)
            part = part_ref[B + i * W : B + (i + 1) * W, :] if i < early else last
            right_ref[to, :] = base_right[to, :] + 0.1 * part
    to = pl.ds(pl.multiple_of(at_ref[2 + 2 * early + 1], W), W)
    right_ref[to, :] = base_right[to, :]


def sum_up(at, base_left, base_right, keep, got, own, last):
    out = jax.ShapeDtypeStruct(base_left.shape, f32)
    return pl.pallas_call(
        sum_kernel,
        out_shape=(out, out),
        in_specs=[SMEM] + [VMEM] * 6,
        out_specs=(VMEM, VMEM),
        scratch_shapes=[pltpu.VMEM((W, W), bf16)],
        compiler_params=PARAMS,
        cost_estimate=pl.CostEstimate(flops=WEIGHT, bytes_accessed=2**22, transcendentals=0),
    )(at, base_left, base_right, keep, got, own, last)


def finish_kernel(at_ref, left_ref, right_ref, own_ref, last_ref, out_ref, result, rows, sems):
    result[1] = right_ref[...]
    to = pl.ds(pl.multiple_of(at_ref[2 + 2 * (FIRST + SECOND) + 1], W), W)
    result[1, to, :] = right_ref[to, :] + 0.1 * right_of(last_ref[...], own_ref[...])
    copies = [pltpu.make_async_copy(result.at[1], out_ref.at[1], sems.at[0])]
    copies[0].start()
    rows[...] = last_ref[pl.ds(pl.multiple_of(at_ref[0], W), W), :]
    for i, start in enumerate(range(0, B, STRIP)):
        to = slice(start, start + STRIP)
        result[0, to, :] = left_ref[to, :] + 0.1 * left_of(last_ref, rows, start)
        copies.append(
            pltpu.make_async_copy(
                result.at[0, pl.ds(start, STRIP)], out_ref.at[0, pl.ds(start, STRIP)], sems.at[1 + i]
            )
        )
        copies[-1].start()
    for copy in copies:
        copy.wait()


def finish(at, left, right, own, last):
    return pl.pallas_call(
        finish_kernel,
        out_shape=jax.ShapeDtypeStruct((2, *left.shape), f32),
        in_specs=[SMEM] + [VMEM] * 4,
        out_specs=pl.BlockSpec(memory_space=pl.ANY),
        scratch_shapes=[
            pltpu.VMEM((2, *left.shape), f32),
            pltpu.VMEM((W, W), bf16),
            pltpu.SemaphoreType.DMA((1 + B // STRIP,)),
        ],
        compiler_params=PARAMS,
    )(at, left, right, own, last)


def ring(value, direction):
    pairs = [
        (x * 2 + core, (x + direction * (1 - 2 * core)) % 4 * 2 + core)
        for x in range(4)
        for core in range(2)
    ]
    return lax.ppermute(value, ("x", "core"), pairs)


def swap(value, axis):
    return lax.ppermute(value, axis, [(0, 1), (1, 0)])


def shards(grad, owner, codes, scale_ids, scale_table):
    rows_here, width_here = grad.shape
    slots = lax.axis_size("tensor")
    y, x, core = (lax.axis_index(name) for name in ("y", "x", "core"))
    chunks = grad.reshape(slots, rows_here // slots, width_here)
    spread = lax.all_to_all(chunks, "tensor", 0, 0, tiled=True)
    owner_row = lax.dynamic_index_in_dim(owner, lax.axis_index("c"), 0, keepdims=False)
    placed = place(spread, owner_row)
    own = lax.all_to_all(placed, "tensor", 0, 0, tiled=True).reshape(rows_here, width_here)
    base_left, base_right = (dequant(side, scale_table, codes, scale_ids) for side in range(2))

    def row_starts(core):
        step = 1 - 2 * core
        xs = [x, x - step, x + step, x, x - step, x + step, x + 2, x + 2]
        ys = [y, y, y, 1 - y, 1 - y, 1 - y, y, 1 - y]
        return [((row * 4 + column % 4) * 2 + core) * W for row, column in zip(ys, xs)]

    mine, theirs = row_starts(core), row_starts(1 - core)
    at = jnp.stack([mine[0], theirs[0]] + mine + theirs).astype(jnp.int32)
    across = swap(own, "y")
    behind = ring(own, 1)
    ahead = ring(own, -1)
    other = swap(own, "core")
    across, base_left = lax.optimization_barrier((across, base_left))
    across_ahead = ring(across, -1)
    behind, base_left = lax.optimization_barrier((behind, base_left))
    across_behind = swap(behind, "y")
    ahead, other, behind = lax.optimization_barrier((ahead, other, behind))
    far = ring(ahead, -1)
    left = first_grams(at, [own, behind, ahead, across])
    left, across_ahead = lax.optimization_barrier((left, across_ahead))
    across_far = ring(across_ahead, -1)
    right = middle_grams(own, other, [own, behind, ahead, across, across_behind])
    keep, send = second_grams(at, own, other, left, right, [across_behind, across_ahead, far])
    got, got_far = swap(send, "core"), swap(across_far, "core")
    left, right = sum_up(at, base_left, base_right, keep, got, own, across_far)
    return finish(at, left, right, own, got_far)


def solution(mesh):
    fine = Mesh(mesh.devices.reshape(4, 2, 4, 2, 8), ("c", "y", "x", "core", "tensor"))
    fsdp = ("c", "y", "x", "core")
    in_specs = (P("tensor", fsdp), P(), P(None, "tensor", fsdp), P(None, "tensor", fsdp), P())
    out_specs = P(None, "tensor", fsdp)
    return jax.shard_map(shards, mesh=fine, in_specs=in_specs, out_specs=out_specs, check_vma=False)
```

time: 101 us -> 97.7 us (0.967)
  waiting for transfers between devices: 30.5 us -> 22.6 us
  Pallas kernels: 8.68 us -> 10.9 us
  starting transfers between devices: 39.9 us -> 42 us
    ppermute x5, waiting for transfers between devices: 8.69 us -> 1.39 us  [swap(): return lax.ppermute(value, axis, [(0, 1), (1, 0)])]
    pallas_call x2 -> x5, Pallas kernels: 3.78 us -> 5.98 us  [the longest x1 2.24 us: finish(): pl.pallas_call(finish_kernel, out_shape=jax.ShapeDtypeStruct((2, *left.sh...]
    ppermute x5, starting transfers between devices: 12 us -> 14 us  [ring(): return lax.ppermute(value, ('x', 'core'), pairs)]
  transfers between devices with their start and end apart: 11 -> 11, of which waited for: 7 -> 7; matrix products, arithmetic and copies ran while one was open for 0% -> 0% of each run, Pallas kernels for 5% -> 8%
where the time goes in v4:
time: 97.7 us; the launch traced here: 97.1 us
  starting transfers between devices  42 us (43%)
  waiting for transfers between devices  22.6 us (23%)
  blocking collectives  20.3 us (21%)
  Pallas kernels  10.9 us (11%)
  local copies, waits for them, and re-layouts  1.1 us (1%)
    all_to_all x1, blocking collectives, shards(): lax.all_to_all(placed, 'tensor', 0, 0, tiled=True)  20.3 us
    all_to_all x1, waiting for transfers between devices, shards(): spread = lax.all_to_all(chunks, 'tensor', 0, 0, tiled=True)  17.9 us
    ppermute x5, starting transfers between devices, swap(): return lax.ppermute(value, axis, [(0, 1), (1, 0)])  17 us
    ppermute x5, starting transfers between devices, ring(): return lax.ppermute(value, ('x', 'core'), pairs)  14 us
    all_to_all x1, starting transfers between devices, shards(): spread = lax.all_to_all(chunks, 'tensor', 0, 0, tiled=True)  11 us
    ppermute x5, waiting for transfers between devices, ring(): return lax.ppermute(value, ('x', 'core'), pairs)  3.23 us
    pallas_call x1, Pallas kernels, second_grams(): pl.pallas_call(second_kernel, out_shape=(out, out), in_specs=[SMEM] + [VM...  2.69 us
    pallas_call x1, Pallas kernels, finish(): pl.pallas_call(finish_kernel, out_shape=jax.ShapeDtypeStruct((2, *left.sh...  2.24 us
  transfers between devices with their start and end apart: 11, of which 7 were waited for; matrix products, arithmetic and copies ran while one was open for 0% of the time, Pallas kernels for 8%

profile of v4, /device:TPU:1, one launch (start us, length us, event | category | flops | bytes accessed | tf_op | source)
XLA Modules:
  0.0 97.1 jit_solution(379163644312158397)
XLA Ops:
  0.0 0.0 copy-start
  0.0 0.0 copy-start.3
  0.0 0.0 copy-start.4
  0.0 11.0 %all-to-all-start = ((bf16[8,256,128]{2,1,0:T(8,128)(2,1)}), bf16[8,256,128]{2,1,0:T(8,128)(2,1)S(1)}, u32[]{:S(2)}, u32[]{:S(2)}) async-start(bf16[8,256,128]{2,1,0:T(8,128)(2,1)} %bitcast.30), calls=%async_computation | async-start | bytes 1048576 | tf_op jit(solution)/shard_map/all_to_all | solution.py:244
  11.0 0.0 copy-done
  11.0 17.9 %all-to-all-done.in_ref = bf16[8,256,128]{2,1,0:T(8,128)(2,1)S(1)} async-done(((bf16[8,256,128]{2,1,0:T(8,128)(2,1)}), bf16[8,256,128]{2,1,0:T(8,128)(2,1)S(1)}, u32[]{:S(2)}, u32[]{:S(2)}) %all-to-all-start) | async-done | bytes 524320 | tf_op jit(solution)/shard_map/all_to_all | solution.py:244
  29.0 0.0 copy-start.1
  29.0 0.6 shard_map.55
  29.6 20.3 %all_to_all.10 = bf16[8,256,128]{2,1,0:T(8,128)(2,1)S(1)} all-to-all(bf16[8,256,128]{2,1,0:T(8,128)(2,1)S(1)} %shard_map.55), channel_id=1, replica_groups=mesh['c'=4,'y'=2,'x'=4,'core'=2,'tensor'=8] {'tensor'}, dimensions={0} | all-to-all | bytes 1048576 | tf_op jit(solution)/shard_map/all_to_all | solution.py:247
  49.8 3.2 %collective-permute-start.1 = (bf16[2048,128]{1,0:T(8,128)(2,1)S(1)}, bf16[2048,128]{1,0:T(8,128)(2,1)S(1)}, u32[]{:S(2)}, u32[]{:S(2)}) collective-permute-start(bf16[2048,128]{1,0:T(8,128)(2,1)S(1)} %bitcast.20), channel_id=1, source_target_pairs={{0,64},{64,0},{1,65},{65,1},{2,66},{66,2},{3,67},{67,3},{4,68},{68... | collective-permute-start | bytes 1572872 | tf_op jit(solution)/shard_map/ppermute | solution.py:236
  53.0 4.4 %collective-permute-start = (bf16[2048,128]{1,0:T(8,128)(2,1)S(1)}, bf16[2048,128]{1,0:T(8,128)(2,1)S(1)}, u32[]{:S(2)}, u32[]{:S(2)}) collective-permute-start(bf16[2048,128]{1,0:T(8,128)(2,1)S(1)} %bitcast.21), channel_id=1, source_target_pairs={{0,16},{8,56},{16,32},{24,8},{32,48},{40,24},{48,0},{56,40},{1,17}... | collective-permute-start | bytes 1572872 | tf_op jit(solution)/shard_map/ppermute | solution.py:232
  57.4 1.9 %collective-permute-start.2 = (bf16[2048,128]{1,0:T(8,128)(2,1)S(1)}, bf16[2048,128]{1,0:T(8,128)(2,1)S(1)}, u32[]{:S(2)}, u32[]{:S(2)}) collective-permute-start(bf16[2048,128]{1,0:T(8,128)(2,1)S(1)} %bitcast.22), channel_id=1, source_target_pairs={{0,48},{8,24},{16,0},{24,40},{32,16},{40,56},{48,32},{56,8},{1,49}... | collective-permute-start | bytes 1572872 | tf_op jit(solution)/shard_map/ppermute | solution.py:232
  59.4 3.7 %collective-permute-start.3 = (bf16[2048,128]{1,0:T(8,128)(2,1)S(1)}, bf16[2048,128]{1,0:T(8,128)(2,1)S(1)}, u32[]{:S(2)}, u32[]{:S(2)}) collective-permute-start(bf16[2048,128]{1,0:T(8,128)(2,1)S(1)} %bitcast.23), channel_id=1, source_target_pairs={{0,8},{8,0},{1,9},{9,1},{2,10},{10,2},{3,11},{11,3},{4,12},{12,4},... | collective-permute-start | bytes 1572872 | tf_op jit(solution)/shard_map/ppermute | solution.py:236
  63.0 0.0 copy-done.3
  63.0 0.0 copy-done.4
  63.0 0.0 copy-done.1
  63.0 0.7 shard_map.56.base_left
  63.8 0.0 copy-start.5
  63.8 1.0 copy-done.5
  64.8 0.0 collective-permute-done.1.refs_3_
  64.8 2.8 %collective-permute-start.4 = (bf16[2048,128]{1,0:T(8,128)(2,1)S(1)}, bf16[2048,128]{1,0:T(8,128)(2,1)}, u32[]{:S(2)}, u32[]{:S(2)}) collective-permute-start(bf16[2048,128]{1,0:T(8,128)(2,1)S(1)} %collective-permute-done.1.refs_3_), channel_id=1, source_target_pairs={{0,48},{8,24},{16,0},{24,40},{32,16},{40,56},{48,32},{56,8},{1,49}... | collective-permute-start | bytes 1572872 | tf_op jit(solution)/shard_map/ppermute | solution.py:232
  67.6 0.0 collective-permute-done.refs_1_
  67.6 3.2 %collective-permute-start.5 = (bf16[2048,128]{1,0:T(8,128)(2,1)S(1)}, bf16[2048,128]{1,0:T(8,128)(2,1)S(1)}, u32[]{:S(2)}, u32[]{:S(2)}) collective-permute-start(bf16[2048,128]{1,0:T(8,128)(2,1)S(1)} %collective-permute-done.refs_1_), channel_id=1, source_target_pairs={{0,64},{64,0},{1,65},{65,1},{2,66},{66,2},{3,67},{67,3},{4,68},{68... | collective-permute-start | bytes 1572872 | tf_op jit(solution)/shard_map/ppermute | solution.py:236
  70.8 0.5 collective-permute-done.2.refs_2_
  71.2 0.0 collective-permute-done.3.other_ref
  71.2 2.7 %collective-permute-start.6 = (bf16[2048,128]{1,0:T(8,128)(2,1)S(1)}, bf16[2048,128]{1,0:T(8,128)(2,1)}, u32[]{:S(2)}, u32[]{:S(2)}) collective-permute-start(bf16[2048,128]{1,0:T(8,128)(2,1)S(1)} %collective-permute-done.2.refs_2_), channel_id=1, source_target_pairs={{0,48},{8,24},{16,0},{24,40},{32,16},{40,56},{48,32},{56,8},{1,49}... | collective-permute-start | bytes 1572872 | tf_op jit(solution)/shard_map/ppermute | solution.py:232
  74.1 0.1 stack.69.at_ref
  74.2 1.6 %shard_map.58.left_ref = f32[2048,256]{1,0:T(8,128)S(1)} custom-call(s32[18]{0:T(128)S(1)} %stack.69.at_ref, bf16[2048,128]{1,0:T(8,128)(2,1)S(1)} %bitcast.24, bf16[2048,128]{1,0:T(8,128)(2,1)S(1)} %collective-permute-done.refs_1_, bf16[2048,128]{1,0:T(8,128)(2,1)S(1)} %collective-permute-done.2.refs_2_, bf16[2048,128]{1,0:T(8,128)(2,1)S(1)} %collective-permute-done.1.refs_3_), custom_call_target="tpu_custom_call" | custom-call | flops 1073741824 | bytes 4194304 | tf_op jit(solution)/shard_map/pallas_call | solution.py:93
  75.8 1.2 %collective-permute-done.4.refs_1_ = bf16[2048,128]{1,0:T(8,128)(2,1)} collective-permute-done((bf16[2048,128]{1,0:T(8,128)(2,1)S(1)}, bf16[2048,128]{1,0:T(8,128)(2,1)}, u32[]{:S(2)}, u32[]{:S(2)}) %collective-permute-start.4) | collective-permute-done | bytes 524320 | tf_op jit(solution)/shard_map/ppermute | solution.py:232
  77.0 2.2 %collective-permute-start.8 = (bf16[2048,128]{1,0:T(8,128)(2,1)}, bf16[2048,128]{1,0:T(8,128)(2,1)S(1)}, u32[]{:S(2)}, u32[]{:S(2)}) collective-permute-start(bf16[2048,128]{1,0:T(8,128)(2,1)} %collective-permute-done.4.refs_1_), channel_id=1, source_target_pairs={{0,48},{8,24},{16,0},{24,40},{32,16},{40,56},{48,32},{56,8},{1,49}... | collective-permute-start | bytes 1572872 | tf_op jit(solution)/shard_map/ppermute | solution.py:232
  79.2 0.7 collective-permute-done.5.refs_4_.refs_0_
  79.8 1.1 %shard_map.59.right_ref = f32[640,256]{1,0:T(8,128)S(1)} custom-call(bf16[2048,128]{1,0:T(8,128)(2,1)S(1)} %bitcast.25, bf16[2048,128]{1,0:T(8,128)(2,1)S(1)} %collective-permute-done.3.other_ref, bf16[2048,128]{1,0:T(8,128)(2,1)S(1)} %bitcast.26, bf16[2048,128]{1,0:T(8,128)(2,1)S(1)} %collective-permute-done.refs_1_, ...), custom_call_target="tpu_custom_call" | custom-call | flops 1073741824 | bytes 4194304 | tf_op jit(solution)/shard_map/pallas_call | solution.py:113
  81.0 0.0 copy-start.2
  81.0 1.6 %collective-permute-done.6.refs_2_ = bf16[2048,128]{1,0:T(8,128)(2,1)} collective-permute-done((bf16[2048,128]{1,0:T(8,128)(2,1)S(1)}, bf16[2048,128]{1,0:T(8,128)(2,1)}, u32[]{:S(2)}, u32[]{:S(2)}) %collective-permute-start.6) | collective-permute-done | bytes 524320 | tf_op jit(solution)/shard_map/ppermute | solution.py:232
  82.6 2.7 %shard_map.60 = (f32[2944,128]{1,0:T(8,128)S(1)}, f32[2944,128]{1,0:T(8,128)S(1)}) custom-call(s32[18]{0:T(128)S(1)} %stack.69.at_ref, bf16[2048,128]{1,0:T(8,128)(2,1)S(1)} %bitcast.27, bf16[2048,128]{1,0:T(8,128)(2,1)S(1)} %collective-permute-done.3.other_ref, f32[2048,256]{1,0:T(8,128)S(1)} %shard_map.58.left_ref, f32[640,256]{1,0:T(8,128)S(1)} %shard_map.59.right_ref, ...), custom_call_target="tpu_custom_call" | custom-call | flops 1073741824 | bytes 4194304 | tf_op jit(solution)/shard_map/pallas_call | solution.py:146
  85.3 0.0 copy-start.6
  85.3 5.0 %collective-permute-start.7 = (f32[2944,128]{1,0:T(8,128)S(1)}, f32[2944,128]{1,0:T(8,128)S(1)}, u32[]{:S(2)}, u32[]{:S(2)}) collective-permute-start(f32[2944,128]{1,0:T(8,128)S(1)} %get-tuple-element.28), channel_id=1, source_target_pairs={{0,8},{8,0},{1,9},{9,1},{2,10},{10,2},{3,11},{11,3},{4,12},{12,4},... | collective-permute-start | bytes 4521992 | tf_op jit(solution)/shard_map/ppermute | solution.py:236
  90.3 0.0 copy-done.2
  90.3 0.7 shard_map.57.base_right
  91.1 0.0 collective-permute-done.8.last_ref
  91.1 1.9 %collective-permute-start.9 = (bf16[2048,128]{1,0:T(8,128)(2,1)S(1)}, bf16[2048,128]{1,0:T(8,128)(2,1)S(1)}, u32[]{:S(2)}, u32[]{:S(2)}) collective-permute-start(bf16[2048,128]{1,0:T(8,128)(2,1)S(1)} %collective-permute-done.8.last_ref), channel_id=1, source_target_pairs={{0,8},{8,0},{1,9},{9,1},{2,10},{10,2},{3,11},{11,3},{4,12},{12,4},... | collective-permute-start | bytes 1572872 | tf_op jit(solution)/shard_map/ppermute | solution.py:236
  93.0 0.2 collective-permute-done.7.got_ref
  93.2 0.0 copy-done.6
  93.3 1.2 %shard_map.61 = (f32[2048,128]{1,0:T(8,128)S(1)}, f32[2048,128]{1,0:T(8,128)S(1)}) custom-call(s32[18]{0:T(128)S(1)} %stack.69.at_ref, f32[2048,128]{1,0:T(8,128)S(1)} %copy-done.6, f32[2048,128]{1,0:T(8,128)S(1)} %shard_map.57.base_right, f32[2944,128]{1,0:T(8,128)S(1)} %get-tuple-element.27.keep_ref, f32[2944,128]{1,0:T(8,128)S(1)} %collective-permute-done.7.got_ref, ...), custom_call_target="tpu_custom_call" | custom-call | flops 68719476736 | bytes 4194304 | tf_op jit(solution)/shard_map/pallas_call | solution.py:180
  94.4 0.5 collective-permute-done.9.last_ref
  94.9 2.2 %shard_map.62 = f32[2,2048,128]{2,1,0:T(8,128)} custom-call(s32[18]{0:T(128)S(1)} %stack.69.at_ref, f32[2048,128]{1,0:T(8,128)S(1)} %get-tuple-element.29.left_ref, f32[2048,128]{1,0:T(8,128)S(1)} %get-tuple-element.30.right_ref, bf16[2048,128]{1,0:T(8,128)(2,1)S(1)} %bitcast.29, bf16[2048,128]{1,0:T(8,128)(2,1)S(1)} %collective-permute-done.9.last_ref), custom_call_target="tpu_custom_call" | custom-call | tf_op jit(solution)/shard_map/pallas_call | solution.py:212
  (1 shorter events, 0.0 us)
Async XLA Ops:
  0.0 11.0 %copy-start = (s32[4,8]{1,0:T(4,128)S(1)}, s32[4,8]{1,0:T(4,128)}, u32[]{:S(2)}) copy-start(s32[4,8]{1,0:T(4,128)} %param.6) | copy-start | bytes 388
  0.0 63.0 %copy-start.3 = (s32[2,16,128]{2,1,0:T(8,128)S(1)}, s32[2,16,128]{2,1,0:T(8,128)}, u32[]{:S(2)}) copy-start(s32[2,16,128]{2,1,0:T(8,128)} %ids_ref.3) | copy-start | bytes 49156
  0.0 63.0 %copy-start.4 = (f32[16]{0:T(128)S(1)}, f32[16]{0:T(128)}, u32[]{:S(2)}) copy-start(f32[16]{0:T(128)} %table_ref.3) | copy-start | bytes 196
  0.0 29.0 %all-to-all-start = ((bf16[8,256,128]{2,1,0:T(8,128)(2,1)}), bf16[8,256,128]{2,1,0:T(8,128)(2,1)S(1)}, u32[]{:S(2)}, u32[]{:S(2)}) async-start(bf16[8,256,128]{2,1,0:T(8,128)(2,1)} %bitcast.30), calls=%async_computation | async-start | bytes 1048576 | tf_op jit(solution)/shard_map/all_to_all | solution.py:244
  29.0 34.1 %copy-start.1 = (s32[2,2048,128]{2,1,0:T(8,128)S(1)}, s32[2,2048,128]{2,1,0:T(8,128)}, u32[]{:S(2)}) copy-start(s32[2,2048,128]{2,1,0:T(8,128)} %codes_ref.3) | copy-start | bytes 6291460
  49.8 14.9 %collective-permute-start.1 = (bf16[2048,128]{1,0:T(8,128)(2,1)S(1)}, bf16[2048,128]{1,0:T(8,128)(2,1)S(1)}, u32[]{:S(2)}, u32[]{:S(2)}) collective-permute-start(bf16[2048,128]{1,0:T(8,128)(2,1)S(1)} %bitcast.20), channel_id=1, source_target_pairs={{0,64},{64,0},{1,65},{65,1},{2,66},{66,2},{3,67},{67,3},{4,68},{68... | collective-permute-start | bytes 1572872 | tf_op jit(solution)/shard_map/ppermute | solution.py:236
  53.0 14.5 %collective-permute-start = (bf16[2048,128]{1,0:T(8,128)(2,1)S(1)}, bf16[2048,128]{1,0:T(8,128)(2,1)S(1)}, u32[]{:S(2)}, u32[]{:S(2)}) collective-permute-start(bf16[2048,128]{1,0:T(8,128)(2,1)S(1)} %bitcast.21), channel_id=1, source_target_pairs={{0,16},{8,56},{16,32},{24,8},{32,48},{40,24},{48,0},{56,40},{1,17}... | collective-permute-start | bytes 1572872 | tf_op jit(solution)/shard_map/ppermute | solution.py:232
  57.4 13.8 %collective-permute-start.2 = (bf16[2048,128]{1,0:T(8,128)(2,1)S(1)}, bf16[2048,128]{1,0:T(8,128)(2,1)S(1)}, u32[]{:S(2)}, u32[]{:S(2)}) collective-permute-start(bf16[2048,128]{1,0:T(8,128)(2,1)S(1)} %bitcast.22), channel_id=1, source_target_pairs={{0,48},{8,24},{16,0},{24,40},{32,16},{40,56},{48,32},{56,8},{1,49}... | collective-permute-start | bytes 1572872 | tf_op jit(solution)/shard_map/ppermute | solution.py:232
  59.4 11.9 %collective-permute-start.3 = (bf16[2048,128]{1,0:T(8,128)(2,1)S(1)}, bf16[2048,128]{1,0:T(8,128)(2,1)S(1)}, u32[]{:S(2)}, u32[]{:S(2)}) collective-permute-start(bf16[2048,128]{1,0:T(8,128)(2,1)S(1)} %bitcast.23), channel_id=1, source_target_pairs={{0,8},{8,0},{1,9},{9,1},{2,10},{10,2},{3,11},{11,3},{4,12},{12,4},... | collective-permute-start | bytes 1572872 | tf_op jit(solution)/shard_map/ppermute | solution.py:236
  63.8 1.0 %copy-start.5 = (f32[2048,128]{1,0:T(8,128)}, f32[2048,128]{1,0:T(8,128)S(1)}, u32[]{:S(2)}) copy-start(f32[2048,128]{1,0:T(8,128)S(1)} %shard_map.56.base_left) | copy-start | bytes 3145732
  64.8 12.2 %collective-permute-start.4 = (bf16[2048,128]{1,0:T(8,128)(2,1)S(1)}, bf16[2048,128]{1,0:T(8,128)(2,1)}, u32[]{:S(2)}, u32[]{:S(2)}) collective-permute-start(bf16[2048,128]{1,0:T(8,128)(2,1)S(1)} %collective-permute-done.1.refs_3_), channel_id=1, source_target_pairs={{0,48},{8,24},{16,0},{24,40},{32,16},{40,56},{48,32},{56,8},{1,49}... | collective-permute-start | bytes 1572872 | tf_op jit(solution)/shard_map/ppermute | solution.py:232
  67.6 12.3 %collective-permute-start.5 = (bf16[2048,128]{1,0:T(8,128)(2,1)S(1)}, bf16[2048,128]{1,0:T(8,128)(2,1)S(1)}, u32[]{:S(2)}, u32[]{:S(2)}) collective-permute-start(bf16[2048,128]{1,0:T(8,128)(2,1)S(1)} %collective-permute-done.refs_1_), channel_id=1, source_target_pairs={{0,64},{64,0},{1,65},{65,1},{2,66},{66,2},{3,67},{67,3},{4,68},{68... | collective-permute-start | bytes 1572872 | tf_op jit(solution)/shard_map/ppermute | solution.py:236
  71.2 11.3 %collective-permute-start.6 = (bf16[2048,128]{1,0:T(8,128)(2,1)S(1)}, bf16[2048,128]{1,0:T(8,128)(2,1)}, u32[]{:S(2)}, u32[]{:S(2)}) collective-permute-start(bf16[2048,128]{1,0:T(8,128)(2,1)S(1)} %collective-permute-done.2.refs_2_), channel_id=1, source_target_pairs={{0,48},{8,24},{16,0},{24,40},{32,16},{40,56},{48,32},{56,8},{1,49}... | collective-permute-start | bytes 1572872 | tf_op jit(solution)/shard_map/ppermute | solution.py:232
  77.0 14.1 %collective-permute-start.8 = (bf16[2048,128]{1,0:T(8,128)(2,1)}, bf16[2048,128]{1,0:T(8,128)(2,1)S(1)}, u32[]{:S(2)}, u32[]{:S(2)}) collective-permute-start(bf16[2048,128]{1,0:T(8,128)(2,1)} %collective-permute-done.4.refs_1_), channel_id=1, source_target_pairs={{0,48},{8,24},{16,0},{24,40},{32,16},{40,56},{48,32},{56,8},{1,49}... | collective-permute-start | bytes 1572872 | tf_op jit(solution)/shard_map/ppermute | solution.py:232
  81.0 9.3 %copy-start.2 = (s32[2,2048,128]{2,1,0:T(8,128)S(1)}, s32[2,2048,128]{2,1,0:T(8,128)}, u32[]{:S(2)}) copy-start(s32[2,2048,128]{2,1,0:T(8,128)} %codes_ref.3) | copy-start | bytes 6291460
  85.3 8.0 %copy-start.6 = (f32[2048,128]{1,0:T(8,128)S(1)}, f32[2048,128]{1,0:T(8,128)}, u32[]{:S(2)}) copy-start(f32[2048,128]{1,0:T(8,128)} %copy-done.5) | copy-start | bytes 3145732
  85.3 8.0 %collective-permute-start.7 = (f32[2944,128]{1,0:T(8,128)S(1)}, f32[2944,128]{1,0:T(8,128)S(1)}, u32[]{:S(2)}, u32[]{:S(2)}) collective-permute-start(f32[2944,128]{1,0:T(8,128)S(1)} %get-tuple-element.28), channel_id=1, source_target_pairs={{0,8},{8,0},{1,9},{9,1},{2,10},{10,2},{3,11},{11,3},{4,12},{12,4},... | collective-permute-start | bytes 4521992 | tf_op jit(solution)/shard_map/ppermute | solution.py:236
  91.1 3.8 %collective-permute-start.9 = (bf16[2048,128]{1,0:T(8,128)(2,1)S(1)}, bf16[2048,128]{1,0:T(8,128)(2,1)S(1)}, u32[]{:S(2)}, u32[]{:S(2)}) collective-permute-start(bf16[2048,128]{1,0:T(8,128)(2,1)S(1)} %collective-permute-done.8.last_ref), channel_id=1, source_target_pairs={{0,8},{8,0},{1,9},{9,1},{2,10},{10,2},{3,11},{11,3},{4,12},{12,4},... | collective-permute-start | bytes 1572872 | tf_op jit(solution)/shard_map/ppermute | solution.py:236

commit v5 on v4

--- a/solution.py
+++ b/solution.py
@@ -12,6 +12,7 @@
 W = 128
 FIRST, MIDDLE, SECOND = 4, 5, 3
 STRIP = 512
+ORDERS = ((0, 4, 2, 6, 1, 5, 3, 7), (0, 4, 6, 2, 7, 3, 5, 1))
 WEIGHT = 2**36
 VMEM = pl.BlockSpec(memory_space=pltpu.VMEM)
 SMEM = pl.BlockSpec(memory_space=pltpu.SMEM)
@@ -20,19 +21,31 @@
 bf16 = jnp.bfloat16
 
 
-def place_kernel(slots_ref, in_ref, out_ref):
-    for row_block in range(in_ref.shape[0]):
-        out_ref[pl.ds(slots_ref[row_block], 1)] = in_ref[row_block : row_block + 1]
-
-
-def place(chunks, slots):
+def place_kernel(places_ref, in_ref, out_ref):
+    for i in range(in_ref.shape[0]):
+        out_ref[pl.ds(places_ref[i], 1)] = in_ref[i : i + 1]
+
+
+def place(chunks, places):
     return pl.pallas_call(
         place_kernel,
         out_shape=jax.ShapeDtypeStruct(chunks.shape, chunks.dtype),
         in_specs=[SMEM, VMEM],
         out_specs=VMEM,
         compiler_params=PARAMS,
-    )(slots, chunks)
+    )(places, chunks)
+
+
+def exchange(chunks):
+    groups = [[core * len(order) + z for z in order] for core, order in enumerate(ORDERS)]
+    return lax.all_to_all(chunks, ("core", "tensor"), 0, 0, axis_index_groups=groups, tiled=True)
+
+
+def destinations(owner_row, core):
+    order = jnp.where(core == 0, jnp.asarray(ORDERS[0], jnp.int32), jnp.asarray(ORDERS[1], jnp.int32))
+    places = jnp.arange(order.shape[0], dtype=jnp.int32)
+    slots = jnp.sum(jnp.where(order[:, None] == places, owner_row, 0), axis=1)
+    return jnp.sum(jnp.where(slots[:, None] == order, places, 0), axis=1)
 
 
 def dequant_kernel(table_ref, codes_ref, ids_ref, out_ref):
@@ -241,10 +254,10 @@
     slots = lax.axis_size("tensor")
     y, x, core = (lax.axis_index(name) for name in ("y", "x", "core"))
     chunks = grad.reshape(slots, rows_here // slots, width_here)
-    spread = lax.all_to_all(chunks, "tensor", 0, 0, tiled=True)
+    spread = exchange(chunks)
     owner_row = lax.dynamic_index_in_dim(owner, lax.axis_index("c"), 0, keepdims=False)
-    placed = place(spread, owner_row)
-    own = lax.all_to_all(placed, "tensor", 0, 0, tiled=True).reshape(rows_here, width_here)
+    placed = place(spread, destinations(owner_row, core))
+    own = exchange(placed).reshape(rows_here, width_here)
     base_left, base_right = (dequant(side, scale_table, codes, scale_ids) for side in range(2))
 
     def row_starts(core):

time: 97.7 us -> 92.7 us (0.949)
  waiting for transfers between devices: 22.6 us -> 19.6 us
  blocking collectives: 20.3 us -> 18.5 us
  starting transfers between devices: 42 us -> 40.6 us
  other arithmetic: 0 us -> 1.04 us
    all_to_all x1, waiting for transfers between devices: 17.9 us -> 12.1 us  [exchange(): lax.all_to_all(chunks, ('core', 'tensor'), 0, 0, axis_index_groups=groups...]
    ppermute x5, waiting for transfers between devices: 3.23 us -> 6.95 us  [ring(): return lax.ppermute(value, ('x', 'core'), pairs)]
    ppermute x5, starting transfers between devices: 14 us -> 12 us  [ring(): return lax.ppermute(value, ('x', 'core'), pairs)]
    all_to_all x1, blocking collectives: 20.3 us -> 18.5 us  [exchange(): lax.all_to_all(chunks, ('core', 'tensor'), 0, 0, axis_index_groups=groups...]
  transfers between devices with their start and end apart: 11 -> 11, of which waited for: 7 -> 6; matrix products, arithmetic and copies ran while one was open for 0% -> 1% of each run, Pallas kernels for 8% -> 9%
where the time goes in v5:
time: 92.7 us; the launch traced here: 92.1 us
  starting transfers between devices  40.6 us (44%)
  waiting for transfers between devices  19.6 us (21%)
  blocking collectives  18.5 us (20%)
  Pallas kernels  10.9 us (12%)
  local copies, waits for them, and re-layouts  1.09 us (1%)
  other arithmetic  1.04 us (1%)
    all_to_all x1, blocking collectives, exchange(): lax.all_to_all(chunks, ('core', 'tensor'), 0, 0, axis_index_groups=groups...  18.5 us
    ppermute x5, starting transfers between devices, swap(): return lax.ppermute(value, axis, [(0, 1), (1, 0)])  17.6 us
    all_to_all x1, waiting for transfers between devices, exchange(): lax.all_to_all(chunks, ('core', 'tensor'), 0, 0, axis_index_groups=groups...  12.1 us
    ppermute x5, starting transfers between devices, ring(): return lax.ppermute(value, ('x', 'core'), pairs)  12 us
    all_to_all x1, starting transfers between devices, exchange(): lax.all_to_all(chunks, ('core', 'tensor'), 0, 0, axis_index_groups=groups...  11 us
    ppermute x5, waiting for transfers between devices, ring(): return lax.ppermute(value, ('x', 'core'), pairs)  6.95 us
    pallas_call x1, Pallas kernels, second_grams(): pl.pallas_call(second_kernel, out_shape=(out, out), in_specs=[SMEM] + [VM...  2.68 us
    pallas_call x1, Pallas kernels, finish(): pl.pallas_call(finish_kernel, out_shape=jax.ShapeDtypeStruct((2, *left.sh...  2.24 us
  transfers between devices with their start and end apart: 11, of which 6 were waited for; matrix products, arithmetic and copies ran while one was open for 1% of the time, Pallas kernels for 9%

profile of v5, /device:TPU:1, one launch (start us, length us, event | category | flops | bytes accessed | tf_op | source)
XLA Modules:
  0.0 92.1 jit_solution(7380409422065106333)
XLA Ops:
  0.0 0.0 copy-start
  0.0 0.0 copy-start.3
  0.0 0.0 copy-start.4
  0.0 11.0 %all-to-all-start = ((bf16[8,256,128]{2,1,0:T(8,128)(2,1)}), bf16[8,256,128]{2,1,0:T(8,128)(2,1)S(1)}, u32[]{:S(2)}, u32[]{:S(2)}) async-start(bf16[8,256,128]{2,1,0:T(8,128)(2,1)} %bitcast.30), calls=%async_computation | async-start | bytes 1048576 | tf_op jit(solution)/shard_map/all_to_all | solution.py:41
  11.0 0.0 copy-done
  11.0 0.7 broadcast_select_fusion
  11.7 0.2 select_reduce_fusion.1
  11.9 0.2 select_reduce_fusion.places_ref
  12.1 12.1 %all-to-all-done.in_ref = bf16[8,256,128]{2,1,0:T(8,128)(2,1)S(1)} async-done(((bf16[8,256,128]{2,1,0:T(8,128)(2,1)}), bf16[8,256,128]{2,1,0:T(8,128)(2,1)S(1)}, u32[]{:S(2)}, u32[]{:S(2)}) %all-to-all-start) | async-done | bytes 524320 | tf_op jit(solution)/shard_map/all_to_all | solution.py:41
  24.2 0.6 shard_map.73
  24.8 18.5 %all_to_all.10 = bf16[8,256,128]{2,1,0:T(8,128)(2,1)S(1)} all-to-all(bf16[8,256,128]{2,1,0:T(8,128)(2,1)S(1)} %shard_map.73), channel_id=1, replica_groups={{0,4,2,6,1,5,3,7},{8,12,14,10,15,11,13,9},{16,20,18,22,17,21,19,23},{24..., dimensions={0} | all-to-all | bytes 1048576 | tf_op jit(solution)/shard_map/all_to_all | solution.py:41
  43.3 3.2 %collective-permute-start.1 = (bf16[2048,128]{1,0:T(8,128)(2,1)S(1)}, bf16[2048,128]{1,0:T(8,128)(2,1)S(1)}, u32[]{:S(2)}, u32[]{:S(2)}) collective-permute-start(bf16[2048,128]{1,0:T(8,128)(2,1)S(1)} %bitcast.20), channel_id=1, source_target_pairs={{0,64},{64,0},{1,65},{65,1},{2,66},{66,2},{3,67},{67,3},{4,68},{68... | collective-permute-start | bytes 1572872 | tf_op jit(solution)/shard_map/ppermute | solution.py:249
  46.5 4.4 %collective-permute-start = (bf16[2048,128]{1,0:T(8,128)(2,1)S(1)}, bf16[2048,128]{1,0:T(8,128)(2,1)S(1)}, u32[]{:S(2)}, u32[]{:S(2)}) collective-permute-start(bf16[2048,128]{1,0:T(8,128)(2,1)S(1)} %bitcast.21), channel_id=1, source_target_pairs={{0,16},{8,56},{16,32},{24,8},{32,48},{40,24},{48,0},{56,40},{1,17}... | collective-permute-start | bytes 1572872 | tf_op jit(solution)/shard_map/ppermute | solution.py:245
  50.9 1.9 %collective-permute-start.2 = (bf16[2048,128]{1,0:T(8,128)(2,1)S(1)}, bf16[2048,128]{1,0:T(8,128)(2,1)S(1)}, u32[]{:S(2)}, u32[]{:S(2)}) collective-permute-start(bf16[2048,128]{1,0:T(8,128)(2,1)S(1)} %bitcast.22), channel_id=1, source_target_pairs={{0,48},{8,24},{16,0},{24,40},{32,16},{40,56},{48,32},{56,8},{1,49}... | collective-permute-start | bytes 1572872 | tf_op jit(solution)/shard_map/ppermute | solution.py:245
  52.8 5.9 %collective-permute-start.3 = (bf16[2048,128]{1,0:T(8,128)(2,1)S(1)}, bf16[2048,128]{1,0:T(8,128)(2,1)S(1)}, u32[]{:S(2)}, u32[]{:S(2)}) collective-permute-start(bf16[2048,128]{1,0:T(8,128)(2,1)S(1)} %bitcast.23), channel_id=1, source_target_pairs={{0,8},{8,0},{1,9},{9,1},{2,10},{10,2},{3,11},{11,3},{4,12},{12,4},... | collective-permute-start | bytes 1572872 | tf_op jit(solution)/shard_map/ppermute | solution.py:249
  58.7 0.0 copy-done.3
  58.7 0.0 copy-done.4
  58.7 0.0 copy-done.1
  58.8 0.7 shard_map.74.base_left
  59.5 0.0 copy-start.5
  59.5 1.0 %copy-done.5 = f32[2048,128]{1,0:T(8,128)} copy-done((f32[2048,128]{1,0:T(8,128)}, f32[2048,128]{1,0:T(8,128)S(1)}, u32[]{:S(2)}) %copy-start.5) | copy-done | bytes 1048600
  60.5 0.0 collective-permute-done.1.refs_3_
  60.5 1.9 %collective-permute-start.4 = (bf16[2048,128]{1,0:T(8,128)(2,1)S(1)}, bf16[2048,128]{1,0:T(8,128)(2,1)}, u32[]{:S(2)}, u32[]{:S(2)}) collective-permute-start(bf16[2048,128]{1,0:T(8,128)(2,1)S(1)} %collective-permute-done.1.refs_3_), channel_id=1, source_target_pairs={{0,48},{8,24},{16,0},{24,40},{32,16},{40,56},{48,32},{56,8},{1,49}... | collective-permute-start | bytes 1572872 | tf_op jit(solution)/shard_map/ppermute | solution.py:245
  62.4 0.0 collective-permute-done.refs_1_
  62.4 2.1 %collective-permute-start.5 = (bf16[2048,128]{1,0:T(8,128)(2,1)S(1)}, bf16[2048,128]{1,0:T(8,128)(2,1)S(1)}, u32[]{:S(2)}, u32[]{:S(2)}) collective-permute-start(bf16[2048,128]{1,0:T(8,128)(2,1)S(1)} %collective-permute-done.refs_1_), channel_id=1, source_target_pairs={{0,64},{64,0},{1,65},{65,1},{2,66},{66,2},{3,67},{67,3},{4,68},{68... | collective-permute-start | bytes 1572872 | tf_op jit(solution)/shard_map/ppermute | solution.py:249
  64.5 2.5 %collective-permute-done.2.refs_2_ = bf16[2048,128]{1,0:T(8,128)(2,1)S(1)} collective-permute-done((bf16[2048,128]{1,0:T(8,128)(2,1)S(1)}, bf16[2048,128]{1,0:T(8,128)(2,1)S(1)}, u32[]{:S(2)}, u32[]{:S(2)}) %collective-permute-start.2) | collective-permute-done | bytes 524320 | tf_op jit(solution)/shard_map/ppermute | solution.py:245
  67.0 0.0 collective-permute-done.3.other_ref
  67.0 1.9 %collective-permute-start.6 = (bf16[2048,128]{1,0:T(8,128)(2,1)S(1)}, bf16[2048,128]{1,0:T(8,128)(2,1)}, u32[]{:S(2)}, u32[]{:S(2)}) collective-permute-start(bf16[2048,128]{1,0:T(8,128)(2,1)S(1)} %collective-permute-done.2.refs_2_), channel_id=1, source_target_pairs={{0,48},{8,24},{16,0},{24,40},{32,16},{40,56},{48,32},{56,8},{1,49}... | collective-permute-start | bytes 1572872 | tf_op jit(solution)/shard_map/ppermute | solution.py:245
  69.0 0.1 stack.69.at_ref
  69.1 1.6 %shard_map.76.left_ref = f32[2048,256]{1,0:T(8,128)S(1)} custom-call(s32[18]{0:T(128)S(1)} %stack.69.at_ref, bf16[2048,128]{1,0:T(8,128)(2,1)S(1)} %bitcast.24, bf16[2048,128]{1,0:T(8,128)(2,1)S(1)} %collective-permute-done.refs_1_, bf16[2048,128]{1,0:T(8,128)(2,1)S(1)} %collective-permute-done.2.refs_2_, bf16[2048,128]{1,0:T(8,128)(2,1)S(1)} %collective-permute-done.1.refs_3_), custom_call_target="tpu_custom_call" | custom-call | flops 1073741824 | bytes 4194304 | tf_op jit(solution)/shard_map/pallas_call | solution.py:106
  70.7 1.9 %collective-permute-done.4.refs_1_ = bf16[2048,128]{1,0:T(8,128)(2,1)} collective-permute-done((bf16[2048,128]{1,0:T(8,128)(2,1)S(1)}, bf16[2048,128]{1,0:T(8,128)(2,1)}, u32[]{:S(2)}, u32[]{:S(2)}) %collective-permute-start.4) | collective-permute-done | bytes 524320 | tf_op jit(solution)/shard_map/ppermute | solution.py:245
  72.7 1.9 %collective-permute-start.8 = (bf16[2048,128]{1,0:T(8,128)(2,1)}, bf16[2048,128]{1,0:T(8,128)(2,1)S(1)}, u32[]{:S(2)}, u32[]{:S(2)}) collective-permute-start(bf16[2048,128]{1,0:T(8,128)(2,1)} %collective-permute-done.4.refs_1_), channel_id=1, source_target_pairs={{0,48},{8,24},{16,0},{24,40},{32,16},{40,56},{48,32},{56,8},{1,49}... | collective-permute-start | bytes 1572872 | tf_op jit(solution)/shard_map/ppermute | solution.py:245
  74.6 0.0 collective-permute-done.5.refs_4_.refs_0_
  74.6 1.1 %shard_map.77.right_ref = f32[640,256]{1,0:T(8,128)S(1)} custom-call(bf16[2048,128]{1,0:T(8,128)(2,1)S(1)} %bitcast.25, bf16[2048,128]{1,0:T(8,128)(2,1)S(1)} %collective-permute-done.3.other_ref, bf16[2048,128]{1,0:T(8,128)(2,1)S(1)} %bitcast.26, bf16[2048,128]{1,0:T(8,128)(2,1)S(1)} %collective-permute-done.refs_1_, ...), custom_call_target="tpu_custom_call" | custom-call | flops 1073741824 | bytes 4194304 | tf_op jit(solution)/shard_map/pallas_call | solution.py:126
  75.7 0.0 copy-start.2
  75.8 2.5 %collective-permute-done.6.refs_2_ = bf16[2048,128]{1,0:T(8,128)(2,1)} collective-permute-done((bf16[2048,128]{1,0:T(8,128)(2,1)S(1)}, bf16[2048,128]{1,0:T(8,128)(2,1)}, u32[]{:S(2)}, u32[]{:S(2)}) %collective-permute-start.6) | collective-permute-done | bytes 524320 | tf_op jit(solution)/shard_map/ppermute | solution.py:245
  78.3 2.7 %shard_map.78 = (f32[2944,128]{1,0:T(8,128)S(1)}, f32[2944,128]{1,0:T(8,128)S(1)}) custom-call(s32[18]{0:T(128)S(1)} %stack.69.at_ref, bf16[2048,128]{1,0:T(8,128)(2,1)S(1)} %bitcast.27, bf16[2048,128]{1,0:T(8,128)(2,1)S(1)} %collective-permute-done.3.other_ref, f32[2048,256]{1,0:T(8,128)S(1)} %shard_map.76.left_ref, f32[640,256]{1,0:T(8,128)S(1)} %shard_map.77.right_ref, ...), custom_call_target="tpu_custom_call" | custom-call | flops 1073741824 | bytes 4194304 | tf_op jit(solution)/shard_map/pallas_call | solution.py:159
  81.0 0.0 copy-start.6
  81.0 4.3 %collective-permute-start.7 = (f32[2944,128]{1,0:T(8,128)S(1)}, f32[2944,128]{1,0:T(8,128)S(1)}, u32[]{:S(2)}, u32[]{:S(2)}) collective-permute-start(f32[2944,128]{1,0:T(8,128)S(1)} %get-tuple-element.28), channel_id=1, source_target_pairs={{0,8},{8,0},{1,9},{9,1},{2,10},{10,2},{3,11},{11,3},{4,12},{12,4},... | collective-permute-start | bytes 4521992 | tf_op jit(solution)/shard_map/ppermute | solution.py:249
  85.3 0.0 copy-done.2
  85.3 0.7 shard_map.75.base_right
  86.1 0.0 collective-permute-done.8.last_ref
  86.1 2.1 %collective-permute-start.9 = (bf16[2048,128]{1,0:T(8,128)(2,1)S(1)}, bf16[2048,128]{1,0:T(8,128)(2,1)S(1)}, u32[]{:S(2)}, u32[]{:S(2)}) collective-permute-start(bf16[2048,128]{1,0:T(8,128)(2,1)S(1)} %collective-permute-done.8.last_ref), channel_id=1, source_target_pairs={{0,8},{8,0},{1,9},{9,1},{2,10},{10,2},{3,11},{11,3},{4,12},{12,4},... | collective-permute-start | bytes 1572872 | tf_op jit(solution)/shard_map/ppermute | solution.py:249
  88.2 0.1 collective-permute-done.7.got_ref
  88.2 0.0 copy-done.6
  88.2 1.2 %shard_map.79 = (f32[2048,128]{1,0:T(8,128)S(1)}, f32[2048,128]{1,0:T(8,128)S(1)}) custom-call(s32[18]{0:T(128)S(1)} %stack.69.at_ref, f32[2048,128]{1,0:T(8,128)S(1)} %copy-done.6, f32[2048,128]{1,0:T(8,128)S(1)} %shard_map.75.base_right, f32[2944,128]{1,0:T(8,128)S(1)} %get-tuple-element.27.keep_ref, f32[2944,128]{1,0:T(8,128)S(1)} %collective-permute-done.7.got_ref, ...), custom_call_target="tpu_custom_call" | custom-call | flops 68719476736 | bytes 4194304 | tf_op jit(solution)/shard_map/pallas_call | solution.py:193
  89.4 0.5 collective-permute-done.9.last_ref
  89.9 2.2 %shard_map.80 = f32[2,2048,128]{2,1,0:T(8,128)} custom-call(s32[18]{0:T(128)S(1)} %stack.69.at_ref, f32[2048,128]{1,0:T(8,128)S(1)} %get-tuple-element.29.left_ref, f32[2048,128]{1,0:T(8,128)S(1)} %get-tuple-element.30.right_ref, bf16[2048,128]{1,0:T(8,128)(2,1)S(1)} %bitcast.29, bf16[2048,128]{1,0:T(8,128)(2,1)S(1)} %collective-permute-done.9.last_ref), custom_call_target="tpu_custom_call" | custom-call | tf_op jit(solution)/shard_map/pallas_call | solution.py:225
  (2 shorter events, 0.0 us)
Async XLA Ops:
  0.0 11.0 %copy-start = (s32[4,8]{1,0:T(4,128)S(1)}, s32[4,8]{1,0:T(4,128)}, u32[]{:S(2)}) copy-start(s32[4,8]{1,0:T(4,128)} %param.8) | copy-start | bytes 388
  0.0 58.7 %copy-start.3 = (s32[2,16,128]{2,1,0:T(8,128)S(1)}, s32[2,16,128]{2,1,0:T(8,128)}, u32[]{:S(2)}) copy-start(s32[2,16,128]{2,1,0:T(8,128)} %ids_ref.3) | copy-start | bytes 49156
  0.0 58.7 %copy-start.4 = (f32[16]{0:T(128)S(1)}, f32[16]{0:T(128)}, u32[]{:S(2)}) copy-start(f32[16]{0:T(128)} %table_ref.3) | copy-start | bytes 196
  0.0 24.2 %all-to-all-start = ((bf16[8,256,128]{2,1,0:T(8,128)(2,1)}), bf16[8,256,128]{2,1,0:T(8,128)(2,1)S(1)}, u32[]{:S(2)}, u32[]{:S(2)}) async-start(bf16[8,256,128]{2,1,0:T(8,128)(2,1)} %bitcast.30), calls=%async_computation | async-start | bytes 1048576 | tf_op jit(solution)/shard_map/all_to_all | solution.py:41
  24.2 34.6 %copy-start.1 = (s32[2,2048,128]{2,1,0:T(8,128)S(1)}, s32[2,2048,128]{2,1,0:T(8,128)}, u32[]{:S(2)}) copy-start(s32[2,2048,128]{2,1,0:T(8,128)} %codes_ref.3) | copy-start | bytes 6291460
  43.3 17.2 %collective-permute-start.1 = (bf16[2048,128]{1,0:T(8,128)(2,1)S(1)}, bf16[2048,128]{1,0:T(8,128)(2,1)S(1)}, u32[]{:S(2)}, u32[]{:S(2)}) collective-permute-start(bf16[2048,128]{1,0:T(8,128)(2,1)S(1)} %bitcast.20), channel_id=1, source_target_pairs={{0,64},{64,0},{1,65},{65,1},{2,66},{66,2},{3,67},{67,3},{4,68},{68... | collective-permute-start | bytes 1572872 | tf_op jit(solution)/shard_map/ppermute | solution.py:249
  46.5 15.9 %collective-permute-start = (bf16[2048,128]{1,0:T(8,128)(2,1)S(1)}, bf16[2048,128]{1,0:T(8,128)(2,1)S(1)}, u32[]{:S(2)}, u32[]{:S(2)}) collective-permute-start(bf16[2048,128]{1,0:T(8,128)(2,1)S(1)} %bitcast.21), channel_id=1, source_target_pairs={{0,16},{8,56},{16,32},{24,8},{32,48},{40,24},{48,0},{56,40},{1,17}... | collective-permute-start | bytes 1572872 | tf_op jit(solution)/shard_map/ppermute | solution.py:245
  50.9 16.1 %collective-permute-start.2 = (bf16[2048,128]{1,0:T(8,128)(2,1)S(1)}, bf16[2048,128]{1,0:T(8,128)(2,1)S(1)}, u32[]{:S(2)}, u32[]{:S(2)}) collective-permute-start(bf16[2048,128]{1,0:T(8,128)(2,1)S(1)} %bitcast.22), channel_id=1, source_target_pairs={{0,48},{8,24},{16,0},{24,40},{32,16},{40,56},{48,32},{56,8},{1,49}... | collective-permute-start | bytes 1572872 | tf_op jit(solution)/shard_map/ppermute | solution.py:245
  52.8 14.2 %collective-permute-start.3 = (bf16[2048,128]{1,0:T(8,128)(2,1)S(1)}, bf16[2048,128]{1,0:T(8,128)(2,1)S(1)}, u32[]{:S(2)}, u32[]{:S(2)}) collective-permute-start(bf16[2048,128]{1,0:T(8,128)(2,1)S(1)} %bitcast.23), channel_id=1, source_target_pairs={{0,8},{8,0},{1,9},{9,1},{2,10},{10,2},{3,11},{11,3},{4,12},{12,4},... | collective-permute-start | bytes 1572872 | tf_op jit(solution)/shard_map/ppermute | solution.py:249
  59.5 1.0 %copy-start.5 = (f32[2048,128]{1,0:T(8,128)}, f32[2048,128]{1,0:T(8,128)S(1)}, u32[]{:S(2)}) copy-start(f32[2048,128]{1,0:T(8,128)S(1)} %shard_map.74.base_left) | copy-start | bytes 3145732
  60.5 12.2 %collective-permute-start.4 = (bf16[2048,128]{1,0:T(8,128)(2,1)S(1)}, bf16[2048,128]{1,0:T(8,128)(2,1)}, u32[]{:S(2)}, u32[]{:S(2)}) collective-permute-start(bf16[2048,128]{1,0:T(8,128)(2,1)S(1)} %collective-permute-done.1.refs_3_), channel_id=1, source_target_pairs={{0,48},{8,24},{16,0},{24,40},{32,16},{40,56},{48,32},{56,8},{1,49}... | collective-permute-start | bytes 1572872 | tf_op jit(solution)/shard_map/ppermute | solution.py:245
  62.4 12.2 %collective-permute-start.5 = (bf16[2048,128]{1,0:T(8,128)(2,1)S(1)}, bf16[2048,128]{1,0:T(8,128)(2,1)S(1)}, u32[]{:S(2)}, u32[]{:S(2)}) collective-permute-start(bf16[2048,128]{1,0:T(8,128)(2,1)S(1)} %collective-permute-done.refs_1_), channel_id=1, source_target_pairs={{0,64},{64,0},{1,65},{65,1},{2,66},{66,2},{3,67},{67,3},{4,68},{68... | collective-permute-start | bytes 1572872 | tf_op jit(solution)/shard_map/ppermute | solution.py:249
  67.0 11.3 %collective-permute-start.6 = (bf16[2048,128]{1,0:T(8,128)(2,1)S(1)}, bf16[2048,128]{1,0:T(8,128)(2,1)}, u32[]{:S(2)}, u32[]{:S(2)}) collective-permute-start(bf16[2048,128]{1,0:T(8,128)(2,1)S(1)} %collective-permute-done.2.refs_2_), channel_id=1, source_target_pairs={{0,48},{8,24},{16,0},{24,40},{32,16},{40,56},{48,32},{56,8},{1,49}... | collective-permute-start | bytes 1572872 | tf_op jit(solution)/shard_map/ppermute | solution.py:245
  72.7 13.4 %collective-permute-start.8 = (bf16[2048,128]{1,0:T(8,128)(2,1)}, bf16[2048,128]{1,0:T(8,128)(2,1)S(1)}, u32[]{:S(2)}, u32[]{:S(2)}) collective-permute-start(bf16[2048,128]{1,0:T(8,128)(2,1)} %collective-permute-done.4.refs_1_), channel_id=1, source_target_pairs={{0,48},{8,24},{16,0},{24,40},{32,16},{40,56},{48,32},{56,8},{1,49}... | collective-permute-start | bytes 1572872 | tf_op jit(solution)/shard_map/ppermute | solution.py:245
  75.7 9.6 %copy-start.2 = (s32[2,2048,128]{2,1,0:T(8,128)S(1)}, s32[2,2048,128]{2,1,0:T(8,128)}, u32[]{:S(2)}) copy-start(s32[2,2048,128]{2,1,0:T(8,128)} %codes_ref.3) | copy-start | bytes 6291460
  81.0 7.3 %copy-start.6 = (f32[2048,128]{1,0:T(8,128)S(1)}, f32[2048,128]{1,0:T(8,128)}, u32[]{:S(2)}) copy-start(f32[2048,128]{1,0:T(8,128)} %copy-done.5) | copy-start | bytes 3145732
  81.0 7.3 %collective-permute-start.7 = (f32[2944,128]{1,0:T(8,128)S(1)}, f32[2944,128]{1,0:T(8,128)S(1)}, u32[]{:S(2)}, u32[]{:S(2)}) collective-permute-start(f32[2944,128]{1,0:T(8,128)S(1)} %get-tuple-element.28), channel_id=1, source_target_pairs={{0,8},{8,0},{1,9},{9,1},{2,10},{10,2},{3,11},{11,3},{4,12},{12,4},... | collective-permute-start | bytes 4521992 | tf_op jit(solution)/shard_map/ppermute | solution.py:249
  86.1 3.8 %collective-permute-start.9 = (bf16[2048,128]{1,0:T(8,128)(2,1)S(1)}, bf16[2048,128]{1,0:T(8,128)(2,1)S(1)}, u32[]{:S(2)}, u32[]{:S(2)}) collective-permute-start(bf16[2048,128]{1,0:T(8,128)(2,1)S(1)} %collective-permute-done.8.last_ref), channel_id=1, source_target_pairs={{0,8},{8,0},{1,9},{9,1},{2,10},{10,2},{3,11},{11,3},{4,12},{12,4},... | collective-permute-start | bytes 1572872 | tf_op jit(solution)/shard_map/ppermute | solution.py:249

commit v6 on v5

--- a/solution.py
+++ b/solution.py
@@ -12,7 +12,7 @@
 W = 128
 FIRST, MIDDLE, SECOND = 4, 5, 3
 STRIP = 512
-ORDERS = ((0, 4, 2, 6, 1, 5, 3, 7), (0, 4, 6, 2, 7, 3, 5, 1))
+ORDERS = ((0, 4, 2, 6, 1, 5, 3, 7), (0, 4, 6, 2, 5, 1, 7, 3))
 WEIGHT = 2**36
 VMEM = pl.BlockSpec(memory_space=pltpu.VMEM)
 SMEM = pl.BlockSpec(memory_space=pltpu.SMEM)
@@ -48,31 +48,46 @@
     return jnp.sum(jnp.where(slots[:, None] == order, places, 0), axis=1)
 
 
-def dequant_kernel(table_ref, codes_ref, ids_ref, out_ref):
-    ids = ids_ref[0]
+def scale_kernel(table_ref, ids_ref, out_ref):
+    ids = ids_ref[...]
     scale = jnp.zeros(ids.shape, f32)
     for level in range(table_ref.shape[0]):
         scale = jnp.where(ids == level, table_ref[level], scale)
-    group_rows = codes_ref.shape[1] // ids.shape[0]
-    for group in range(ids.shape[0]):
-        rows = slice(group * group_rows, (group + 1) * group_rows)
-        code = codes_ref[0, rows, :].astype(f32)
-        out_ref[rows, :] = 0.9 * (scale[group : group + 1] * ((code - 7.5) / 7.5))
-
-
-def dequant(side, scale_table, codes, scale_ids):
-    def block(array):
-        return pl.BlockSpec((1, *array.shape[1:]), lambda i: (side, 0, 0))
-
+    out_ref[...] = scale
+
+
+def scales(scale_table, scale_ids):
+    return pl.pallas_call(
+        scale_kernel,
+        out_shape=jax.ShapeDtypeStruct(scale_ids.shape, f32),
+        in_specs=[SMEM, VMEM],
+        out_specs=VMEM,
+        compiler_params=PARAMS,
+        cost_estimate=pl.CostEstimate(flops=WEIGHT, bytes_accessed=2**15, transcendentals=0),
+    )(scale_table, scale_ids)
+
+
+def dequant_kernel(codes_ref, scale_ref, left_ref, right_ref):
+    groups = scale_ref.shape[1]
+    group_rows = codes_ref.shape[1] // groups
+    for side, out_ref in enumerate((left_ref, right_ref)):
+        for group in range(groups):
+            rows = slice(group * group_rows, (group + 1) * group_rows)
+            code = codes_ref[side, rows, :].astype(f32)
+            scale = scale_ref[side, group : group + 1, :]
+            out_ref[rows, :] = 0.9 * (scale * ((code - 7.5) / 7.5))
+
+
+def dequant(codes, scale):
+    out = jax.ShapeDtypeStruct(codes.shape[1:], f32)
     return pl.pallas_call(
         dequant_kernel,
-        grid=(1,),
-        out_shape=jax.ShapeDtypeStruct(codes.shape[1:], f32),
-        in_specs=[SMEM, block(codes), block(scale_ids)],
-        out_specs=pl.BlockSpec(codes.shape[1:], lambda i: (0, 0)),
-        compiler_params=PARAMS,
-        cost_estimate=pl.CostEstimate(flops=WEIGHT, bytes_accessed=2**21, transcendentals=0),
-    )(scale_table, codes, scale_ids)
+        out_shape=(out, out),
+        in_specs=[VMEM, VMEM],
+        out_specs=(VMEM, VMEM),
+        compiler_params=PARAMS,
+        cost_estimate=pl.CostEstimate(flops=WEIGHT, bytes_accessed=2**22, transcendentals=0),
+    )(codes, scale)
 
 
 def left_of(block, rows, start):
@@ -258,7 +273,7 @@
     owner_row = lax.dynamic_index_in_dim(owner, lax.axis_index("c"), 0, keepdims=False)
     placed = place(spread, destinations(owner_row, core))
     own = exchange(placed).reshape(rows_here, width_here)
-    base_left, base_right = (dequant(side, scale_table, codes, scale_ids) for side in range(2))
+    scale = scales(scale_table, scale_ids)
 
     def row_starts(core):
         step = 1 - 2 * core
@@ -272,9 +287,9 @@
     behind = ring(own, 1)
     ahead = ring(own, -1)
     other = swap(own, "core")
-    across, base_left = lax.optimization_barrier((across, base_left))
+    across, scale = lax.optimization_barrier((across, scale))
     across_ahead = ring(across, -1)
-    behind, base_left = lax.optimization_barrier((behind, base_left))
+    behind, scale = lax.optimization_barrier((behind, scale))
     across_behind = swap(behind, "y")
     ahead, other, behind = lax.optimization_barrier((ahead, other, behind))
     far = ring(ahead, -1)
@@ -284,6 +299,7 @@
     right = middle_grams(own, other, [own, behind, ahead, across, across_behind])
     keep, send = second_grams(at, own, other, left, right, [across_behind, across_ahead, far])
     got, got_far = swap(send, "core"), swap(across_far, "core")
+    base_left, base_right = dequant(codes, scale)
     left, right = sum_up(at, base_left, base_right, keep, got, own, across_far)
     return finish(at, left, right, own, got_far)
 

time: 92.7 us -> 92.8 us (level)
  blocking collectives: 18.5 us -> 19.8 us
  local copies, waits for them, and re-layouts: 1.09 us -> 0.12 us
    all_to_all x1, blocking collectives: 18.5 us -> 19.8 us  [exchange(): lax.all_to_all(chunks, ('core', 'tensor'), 0, 0, axis_index_groups=groups...]
    all_to_all x1, waiting for transfers between devices: 12.1 us -> 10.9 us  [exchange(): lax.all_to_all(chunks, ('core', 'tensor'), 0, 0, axis_index_groups=groups...]
    ppermute x5, waiting for transfers between devices: 6.95 us -> 8.08 us  [ring(): return lax.ppermute(value, ('x', 'core'), pairs)]
    unnamed x14 -> x8, local copies, waits for them, and re-layouts: 0.99 us -> 0.02 us
  transfers between devices with their start and end apart: 11 -> 11, of which waited for: 6 -> 5; matrix products, arithmetic and copies ran while one was open for 1% -> 1% of each run, Pallas kernels for 9% -> 8%
where the time goes in v6:
time: 92.8 us; the launch traced here: 92.2 us
  starting transfers between devices  41.2 us (44%)
  blocking collectives  19.8 us (21%)
  waiting for transfers between devices  19.4 us (21%)
  Pallas kernels  10.4 us (11%)
  other arithmetic  1.04 us (1%)
    all_to_all x1, blocking collectives, exchange(): lax.all_to_all(chunks, ('core', 'tensor'), 0, 0, axis_index_groups=groups...  19.8 us
    ppermute x5, starting transfers between devices, swap(): return lax.ppermute(value, axis, [(0, 1), (1, 0)])  18.1 us
    ppermute x5, starting transfers between devices, ring(): return lax.ppermute(value, ('x', 'core'), pairs)  12 us
    all_to_all x1, starting transfers between devices, exchange(): lax.all_to_all(chunks, ('core', 'tensor'), 0, 0, axis_index_groups=groups...  11 us
    all_to_all x1, waiting for transfers between devices, exchange(): lax.all_to_all(chunks, ('core', 'tensor'), 0, 0, axis_index_groups=groups...  10.9 us
    ppermute x5, waiting for transfers between devices, ring(): return lax.ppermute(value, ('x', 'core'), pairs)  8.08 us
    pallas_call x1, Pallas kernels, second_grams(): pl.pallas_call(second_kernel, out_shape=(out, out), in_specs=[SMEM] + [VM...  2.69 us
    pallas_call x1, Pallas kernels, finish(): pl.pallas_call(finish_kernel, out_shape=jax.ShapeDtypeStruct((2, *left.sh...  2.24 us
  transfers between devices with their start and end apart: 11, of which 5 were waited for; matrix products, arithmetic and copies ran while one was open for 1% of the time, Pallas kernels for 8%

profile of v6, /device:TPU:1, one launch (start us, length us, event | category | flops | bytes accessed | tf_op | source)
XLA Modules:
  0.0 92.2 jit_solution(9892506478737985986)
XLA Ops:
  0.0 0.0 copy-start
  0.0 0.0 copy-start.2
  0.0 0.0 copy-start.3
  0.0 11.0 %all-to-all-start = ((bf16[8,256,128]{2,1,0:T(8,128)(2,1)}), bf16[8,256,128]{2,1,0:T(8,128)(2,1)S(1)}, u32[]{:S(2)}, u32[]{:S(2)}) async-start(bf16[8,256,128]{2,1,0:T(8,128)(2,1)} %bitcast.30), calls=%async_computation | async-start | bytes 1048576 | tf_op jit(solution)/shard_map/all_to_all | solution.py:41
  11.0 0.0 copy-done
  11.0 0.7 broadcast_select_fusion
  11.7 0.2 select_reduce_fusion.1
  11.9 0.2 select_reduce_fusion.places_ref
  12.1 10.9 %all-to-all-done.in_ref = bf16[8,256,128]{2,1,0:T(8,128)(2,1)S(1)} async-done(((bf16[8,256,128]{2,1,0:T(8,128)(2,1)}), bf16[8,256,128]{2,1,0:T(8,128)(2,1)S(1)}, u32[]{:S(2)}, u32[]{:S(2)}) %all-to-all-start) | async-done | bytes 524320 | tf_op jit(solution)/shard_map/all_to_all | solution.py:41
  23.0 0.6 shard_map.73
  23.6 19.8 %all_to_all.10 = bf16[8,256,128]{2,1,0:T(8,128)(2,1)S(1)} all-to-all(bf16[8,256,128]{2,1,0:T(8,128)(2,1)S(1)} %shard_map.73), channel_id=1, replica_groups={{0,4,2,6,1,5,3,7},{8,12,14,10,13,9,15,11},{16,20,18,22,17,21,19,23},{24..., dimensions={0} | all-to-all | bytes 1048576 | tf_op jit(solution)/shard_map/all_to_all | solution.py:41
  43.4 3.2 %collective-permute-start.1 = (bf16[2048,128]{1,0:T(8,128)(2,1)S(1)}, bf16[2048,128]{1,0:T(8,128)(2,1)S(1)}, u32[]{:S(2)}, u32[]{:S(2)}) collective-permute-start(bf16[2048,128]{1,0:T(8,128)(2,1)S(1)} %bitcast.20), channel_id=1, source_target_pairs={{0,64},{64,0},{1,65},{65,1},{2,66},{66,2},{3,67},{67,3},{4,68},{68... | collective-permute-start | bytes 1572872 | tf_op jit(solution)/shard_map/ppermute | solution.py:264
  46.6 4.4 %collective-permute-start = (bf16[2048,128]{1,0:T(8,128)(2,1)S(1)}, bf16[2048,128]{1,0:T(8,128)(2,1)S(1)}, u32[]{:S(2)}, u32[]{:S(2)}) collective-permute-start(bf16[2048,128]{1,0:T(8,128)(2,1)S(1)} %bitcast.21), channel_id=1, source_target_pairs={{0,16},{8,56},{16,32},{24,8},{32,48},{40,24},{48,0},{56,40},{1,17}... | collective-permute-start | bytes 1572872 | tf_op jit(solution)/shard_map/ppermute | solution.py:260
  51.0 1.9 %collective-permute-start.2 = (bf16[2048,128]{1,0:T(8,128)(2,1)S(1)}, bf16[2048,128]{1,0:T(8,128)(2,1)S(1)}, u32[]{:S(2)}, u32[]{:S(2)}) collective-permute-start(bf16[2048,128]{1,0:T(8,128)(2,1)S(1)} %bitcast.22), channel_id=1, source_target_pairs={{0,48},{8,24},{16,0},{24,40},{32,16},{40,56},{48,32},{56,8},{1,49}... | collective-permute-start | bytes 1572872 | tf_op jit(solution)/shard_map/ppermute | solution.py:260
  53.0 5.7 %collective-permute-start.3 = (bf16[2048,128]{1,0:T(8,128)(2,1)S(1)}, bf16[2048,128]{1,0:T(8,128)(2,1)S(1)}, u32[]{:S(2)}, u32[]{:S(2)}) collective-permute-start(bf16[2048,128]{1,0:T(8,128)(2,1)S(1)} %bitcast.23), channel_id=1, source_target_pairs={{0,8},{8,0},{1,9},{9,1},{2,10},{10,2},{3,11},{11,3},{4,12},{12,4},... | collective-permute-start | bytes 1572872 | tf_op jit(solution)/shard_map/ppermute | solution.py:264
  58.6 0.0 copy-done.2
  58.7 0.0 copy-done.3
  58.7 0.6 shard_map.74.scale_ref
  59.2 0.0 collective-permute-done.1.refs_3_
  59.3 1.9 %collective-permute-start.4 = (bf16[2048,128]{1,0:T(8,128)(2,1)S(1)}, bf16[2048,128]{1,0:T(8,128)(2,1)}, u32[]{:S(2)}, u32[]{:S(2)}) collective-permute-start(bf16[2048,128]{1,0:T(8,128)(2,1)S(1)} %collective-permute-done.1.refs_3_), channel_id=1, source_target_pairs={{0,48},{8,24},{16,0},{24,40},{32,16},{40,56},{48,32},{56,8},{1,49}... | collective-permute-start | bytes 1572872 | tf_op jit(solution)/shard_map/ppermute | solution.py:260
  61.2 0.0 collective-permute-done.refs_1_
  61.2 2.1 %collective-permute-start.5 = (bf16[2048,128]{1,0:T(8,128)(2,1)S(1)}, bf16[2048,128]{1,0:T(8,128)(2,1)S(1)}, u32[]{:S(2)}, u32[]{:S(2)}) collective-permute-start(bf16[2048,128]{1,0:T(8,128)(2,1)S(1)} %collective-permute-done.refs_1_), channel_id=1, source_target_pairs={{0,64},{64,0},{1,65},{65,1},{2,66},{66,2},{3,67},{67,3},{4,68},{68... | collective-permute-start | bytes 1572872 | tf_op jit(solution)/shard_map/ppermute | solution.py:264
  63.3 3.6 %collective-permute-done.2.refs_2_ = bf16[2048,128]{1,0:T(8,128)(2,1)S(1)} collective-permute-done((bf16[2048,128]{1,0:T(8,128)(2,1)S(1)}, bf16[2048,128]{1,0:T(8,128)(2,1)S(1)}, u32[]{:S(2)}, u32[]{:S(2)}) %collective-permute-start.2) | collective-permute-done | bytes 524320 | tf_op jit(solution)/shard_map/ppermute | solution.py:260
  66.9 0.0 collective-permute-done.3.other_ref
  66.9 1.9 %collective-permute-start.6 = (bf16[2048,128]{1,0:T(8,128)(2,1)S(1)}, bf16[2048,128]{1,0:T(8,128)(2,1)}, u32[]{:S(2)}, u32[]{:S(2)}) collective-permute-start(bf16[2048,128]{1,0:T(8,128)(2,1)S(1)} %collective-permute-done.2.refs_2_), channel_id=1, source_target_pairs={{0,48},{8,24},{16,0},{24,40},{32,16},{40,56},{48,32},{56,8},{1,49}... | collective-permute-start | bytes 1572872 | tf_op jit(solution)/shard_map/ppermute | solution.py:260
  68.9 0.1 stack.69.at_ref
  69.0 1.7 %shard_map.76.left_ref = f32[2048,256]{1,0:T(8,128)S(1)} custom-call(s32[18]{0:T(128)S(1)} %stack.69.at_ref, bf16[2048,128]{1,0:T(8,128)(2,1)S(1)} %bitcast.24, bf16[2048,128]{1,0:T(8,128)(2,1)S(1)} %collective-permute-done.refs_1_, bf16[2048,128]{1,0:T(8,128)(2,1)S(1)} %collective-permute-done.2.refs_2_, bf16[2048,128]{1,0:T(8,128)(2,1)S(1)} %collective-permute-done.1.refs_3_), custom_call_target="tpu_custom_call" | custom-call | flops 1073741824 | bytes 4194304 | tf_op jit(solution)/shard_map/pallas_call | solution.py:121
  70.7 1.9 %collective-permute-done.4.refs_1_ = bf16[2048,128]{1,0:T(8,128)(2,1)} collective-permute-done((bf16[2048,128]{1,0:T(8,128)(2,1)S(1)}, bf16[2048,128]{1,0:T(8,128)(2,1)}, u32[]{:S(2)}, u32[]{:S(2)}) %collective-permute-start.4) | collective-permute-done | bytes 524320 | tf_op jit(solution)/shard_map/ppermute | solution.py:260
  72.6 1.9 %collective-permute-start.8 = (bf16[2048,128]{1,0:T(8,128)(2,1)}, bf16[2048,128]{1,0:T(8,128)(2,1)S(1)}, u32[]{:S(2)}, u32[]{:S(2)}) collective-permute-start(bf16[2048,128]{1,0:T(8,128)(2,1)} %collective-permute-done.4.refs_1_), channel_id=1, source_target_pairs={{0,48},{8,24},{16,0},{24,40},{32,16},{40,56},{48,32},{56,8},{1,49}... | collective-permute-start | bytes 1572872 | tf_op jit(solution)/shard_map/ppermute | solution.py:260
  74.5 0.0 collective-permute-done.5.refs_4_.refs_0_
  74.5 1.1 %shard_map.77.right_ref = f32[640,256]{1,0:T(8,128)S(1)} custom-call(bf16[2048,128]{1,0:T(8,128)(2,1)S(1)} %bitcast.25, bf16[2048,128]{1,0:T(8,128)(2,1)S(1)} %collective-permute-done.3.other_ref, bf16[2048,128]{1,0:T(8,128)(2,1)S(1)} %bitcast.26, bf16[2048,128]{1,0:T(8,128)(2,1)S(1)} %collective-permute-done.refs_1_, ...), custom_call_target="tpu_custom_call" | custom-call | flops 1073741824 | bytes 4194304 | tf_op jit(solution)/shard_map/pallas_call | solution.py:141
  75.7 0.0 copy-start.1
  75.7 2.6 %collective-permute-done.6.refs_2_ = bf16[2048,128]{1,0:T(8,128)(2,1)} collective-permute-done((bf16[2048,128]{1,0:T(8,128)(2,1)S(1)}, bf16[2048,128]{1,0:T(8,128)(2,1)}, u32[]{:S(2)}, u32[]{:S(2)}) %collective-permute-start.6) | collective-permute-done | bytes 524320 | tf_op jit(solution)/shard_map/ppermute | solution.py:260
  78.2 2.7 %shard_map.78 = (f32[2944,128]{1,0:T(8,128)S(1)}, f32[2944,128]{1,0:T(8,128)S(1)}) custom-call(s32[18]{0:T(128)S(1)} %stack.69.at_ref, bf16[2048,128]{1,0:T(8,128)(2,1)S(1)} %bitcast.27, bf16[2048,128]{1,0:T(8,128)(2,1)S(1)} %collective-permute-done.3.other_ref, f32[2048,256]{1,0:T(8,128)S(1)} %shard_map.76.left_ref, f32[640,256]{1,0:T(8,128)S(1)} %shard_map.77.right_ref, ...), custom_call_target="tpu_custom_call" | custom-call | flops 1073741824 | bytes 4194304 | tf_op jit(solution)/shard_map/pallas_call | solution.py:174
  80.9 3.9 %collective-permute-start.7 = (f32[2944,128]{1,0:T(8,128)S(1)}, f32[2944,128]{1,0:T(8,128)S(1)}, u32[]{:S(2)}, u32[]{:S(2)}) collective-permute-start(f32[2944,128]{1,0:T(8,128)S(1)} %get-tuple-element.32), channel_id=1, source_target_pairs={{0,8},{8,0},{1,9},{9,1},{2,10},{10,2},{3,11},{11,3},{4,12},{12,4},... | collective-permute-start | bytes 4521992 | tf_op jit(solution)/shard_map/ppermute | solution.py:264
  84.8 0.0 copy-done.1
  84.8 0.3 shard_map.75
  85.2 0.0 collective-permute-done.8.last_ref
  85.2 3.3 %collective-permute-start.9 = (bf16[2048,128]{1,0:T(8,128)(2,1)S(1)}, bf16[2048,128]{1,0:T(8,128)(2,1)S(1)}, u32[]{:S(2)}, u32[]{:S(2)}) collective-permute-start(bf16[2048,128]{1,0:T(8,128)(2,1)S(1)} %collective-permute-done.8.last_ref), channel_id=1, source_target_pairs={{0,8},{8,0},{1,9},{9,1},{2,10},{10,2},{3,11},{11,3},{4,12},{12,4},... | collective-permute-start | bytes 1572872 | tf_op jit(solution)/shard_map/ppermute | solution.py:264
  88.5 0.0 collective-permute-done.7.got_ref
  88.5 1.2 %shard_map.79 = (f32[2048,128]{1,0:T(8,128)S(1)}, f32[2048,128]{1,0:T(8,128)S(1)}) custom-call(s32[18]{0:T(128)S(1)} %stack.69.at_ref, f32[2048,128]{1,0:T(8,128)S(1)} %get-tuple-element.22.base_left, f32[2048,128]{1,0:T(8,128)S(1)} %get-tuple-element.23.base_right, f32[2944,128]{1,0:T(8,128)S(1)} %get-tuple-element.31.keep_ref, ...), custom_call_target="tpu_custom_call" | custom-call | flops 68719476736 | bytes 4194304 | tf_op jit(solution)/shard_map/pallas_call | solution.py:208
  89.7 0.3 collective-permute-done.9.last_ref
  90.0 2.2 %shard_map.80 = f32[2,2048,128]{2,1,0:T(8,128)} custom-call(s32[18]{0:T(128)S(1)} %stack.69.at_ref, f32[2048,128]{1,0:T(8,128)S(1)} %get-tuple-element.33.left_ref, f32[2048,128]{1,0:T(8,128)S(1)} %get-tuple-element.34.right_ref, bf16[2048,128]{1,0:T(8,128)(2,1)S(1)} %bitcast.29, bf16[2048,128]{1,0:T(8,128)(2,1)S(1)} %collective-permute-done.9.last_ref), custom_call_target="tpu_custom_call" | custom-call | tf_op jit(solution)/shard_map/pallas_call | solution.py:240
  (1 shorter events, 0.0 us)
Async XLA Ops:
  0.0 11.0 %copy-start = (s32[4,8]{1,0:T(4,128)S(1)}, s32[4,8]{1,0:T(4,128)}, u32[]{:S(2)}) copy-start(s32[4,8]{1,0:T(4,128)} %param.8) | copy-start | bytes 388
  0.0 58.6 %copy-start.2 = (s32[2,16,128]{2,1,0:T(8,128)S(1)}, s32[2,16,128]{2,1,0:T(8,128)}, u32[]{:S(2)}) copy-start(s32[2,16,128]{2,1,0:T(8,128)} %ids_ref.1) | copy-start | bytes 49156
  0.0 58.7 %copy-start.3 = (f32[16]{0:T(128)S(1)}, f32[16]{0:T(128)}, u32[]{:S(2)}) copy-start(f32[16]{0:T(128)} %table_ref.1) | copy-start | bytes 196
  0.0 23.0 %all-to-all-start = ((bf16[8,256,128]{2,1,0:T(8,128)(2,1)}), bf16[8,256,128]{2,1,0:T(8,128)(2,1)S(1)}, u32[]{:S(2)}, u32[]{:S(2)}) async-start(bf16[8,256,128]{2,1,0:T(8,128)(2,1)} %bitcast.30), calls=%async_computation | async-start | bytes 1048576 | tf_op jit(solution)/shard_map/all_to_all | solution.py:41
  43.4 15.8 %collective-permute-start.1 = (bf16[2048,128]{1,0:T(8,128)(2,1)S(1)}, bf16[2048,128]{1,0:T(8,128)(2,1)S(1)}, u32[]{:S(2)}, u32[]{:S(2)}) collective-permute-start(bf16[2048,128]{1,0:T(8,128)(2,1)S(1)} %bitcast.20), channel_id=1, source_target_pairs={{0,64},{64,0},{1,65},{65,1},{2,66},{66,2},{3,67},{67,3},{4,68},{68... | collective-permute-start | bytes 1572872 | tf_op jit(solution)/shard_map/ppermute | solution.py:264
  46.6 14.5 %collective-permute-start = (bf16[2048,128]{1,0:T(8,128)(2,1)S(1)}, bf16[2048,128]{1,0:T(8,128)(2,1)S(1)}, u32[]{:S(2)}, u32[]{:S(2)}) collective-permute-start(bf16[2048,128]{1,0:T(8,128)(2,1)S(1)} %bitcast.21), channel_id=1, source_target_pairs={{0,16},{8,56},{16,32},{24,8},{32,48},{40,24},{48,0},{56,40},{1,17}... | collective-permute-start | bytes 1572872 | tf_op jit(solution)/shard_map/ppermute | solution.py:260
  51.0 15.8 %collective-permute-start.2 = (bf16[2048,128]{1,0:T(8,128)(2,1)S(1)}, bf16[2048,128]{1,0:T(8,128)(2,1)S(1)}, u32[]{:S(2)}, u32[]{:S(2)}) collective-permute-start(bf16[2048,128]{1,0:T(8,128)(2,1)S(1)} %bitcast.22), channel_id=1, source_target_pairs={{0,48},{8,24},{16,0},{24,40},{32,16},{40,56},{48,32},{56,8},{1,49}... | collective-permute-start | bytes 1572872 | tf_op jit(solution)/shard_map/ppermute | solution.py:260
  53.0 13.9 %collective-permute-start.3 = (bf16[2048,128]{1,0:T(8,128)(2,1)S(1)}, bf16[2048,128]{1,0:T(8,128)(2,1)S(1)}, u32[]{:S(2)}, u32[]{:S(2)}) collective-permute-start(bf16[2048,128]{1,0:T(8,128)(2,1)S(1)} %bitcast.23), channel_id=1, source_target_pairs={{0,8},{8,0},{1,9},{9,1},{2,10},{10,2},{3,11},{11,3},{4,12},{12,4},... | collective-permute-start | bytes 1572872 | tf_op jit(solution)/shard_map/ppermute | solution.py:264
  59.3 13.3 %collective-permute-start.4 = (bf16[2048,128]{1,0:T(8,128)(2,1)S(1)}, bf16[2048,128]{1,0:T(8,128)(2,1)}, u32[]{:S(2)}, u32[]{:S(2)}) collective-permute-start(bf16[2048,128]{1,0:T(8,128)(2,1)S(1)} %collective-permute-done.1.refs_3_), channel_id=1, source_target_pairs={{0,48},{8,24},{16,0},{24,40},{32,16},{40,56},{48,32},{56,8},{1,49}... | collective-permute-start | bytes 1572872 | tf_op jit(solution)/shard_map/ppermute | solution.py:260
  61.2 13.3 %collective-permute-start.5 = (bf16[2048,128]{1,0:T(8,128)(2,1)S(1)}, bf16[2048,128]{1,0:T(8,128)(2,1)S(1)}, u32[]{:S(2)}, u32[]{:S(2)}) collective-permute-start(bf16[2048,128]{1,0:T(8,128)(2,1)S(1)} %collective-permute-done.refs_1_), channel_id=1, source_target_pairs={{0,64},{64,0},{1,65},{65,1},{2,66},{66,2},{3,67},{67,3},{4,68},{68... | collective-permute-start | bytes 1572872 | tf_op jit(solution)/shard_map/ppermute | solution.py:264
  66.9 11.3 %collective-permute-start.6 = (bf16[2048,128]{1,0:T(8,128)(2,1)S(1)}, bf16[2048,128]{1,0:T(8,128)(2,1)}, u32[]{:S(2)}, u32[]{:S(2)}) collective-permute-start(bf16[2048,128]{1,0:T(8,128)(2,1)S(1)} %collective-permute-done.2.refs_2_), channel_id=1, source_target_pairs={{0,48},{8,24},{16,0},{24,40},{32,16},{40,56},{48,32},{56,8},{1,49}... | collective-permute-start | bytes 1572872 | tf_op jit(solution)/shard_map/ppermute | solution.py:260
  72.6 12.6 %collective-permute-start.8 = (bf16[2048,128]{1,0:T(8,128)(2,1)}, bf16[2048,128]{1,0:T(8,128)(2,1)S(1)}, u32[]{:S(2)}, u32[]{:S(2)}) collective-permute-start(bf16[2048,128]{1,0:T(8,128)(2,1)} %collective-permute-done.4.refs_1_), channel_id=1, source_target_pairs={{0,48},{8,24},{16,0},{24,40},{32,16},{40,56},{48,32},{56,8},{1,49}... | collective-permute-start | bytes 1572872 | tf_op jit(solution)/shard_map/ppermute | solution.py:260
  75.7 9.2 %copy-start.1 = (s32[2,2048,128]{2,1,0:T(8,128)S(1)}, s32[2,2048,128]{2,1,0:T(8,128)}, u32[]{:S(2)}) copy-start(s32[2,2048,128]{2,1,0:T(8,128)} %codes_ref.1) | copy-start | bytes 6291460
  80.9 7.6 %collective-permute-start.7 = (f32[2944,128]{1,0:T(8,128)S(1)}, f32[2944,128]{1,0:T(8,128)S(1)}, u32[]{:S(2)}, u32[]{:S(2)}) collective-permute-start(f32[2944,128]{1,0:T(8,128)S(1)} %get-tuple-element.32), channel_id=1, source_target_pairs={{0,8},{8,0},{1,9},{9,1},{2,10},{10,2},{3,11},{11,3},{4,12},{12,4},... | collective-permute-start | bytes 4521992 | tf_op jit(solution)/shard_map/ppermute | solution.py:264
  85.2 4.8 %collective-permute-start.9 = (bf16[2048,128]{1,0:T(8,128)(2,1)S(1)}, bf16[2048,128]{1,0:T(8,128)(2,1)S(1)}, u32[]{:S(2)}, u32[]{:S(2)}) collective-permute-start(bf16[2048,128]{1,0:T(8,128)(2,1)S(1)} %collective-permute-done.8.last_ref), channel_id=1, source_target_pairs={{0,8},{8,0},{1,9},{9,1},{2,10},{10,2},{3,11},{11,3},{4,12},{12,4},... | collective-permute-start | bytes 1572872 | tf_op jit(solution)/shard_map/ppermute | solution.py:264
